TPU v7x, 256 devices: a whole 4x4x8 slice. The times are simulated.
256 devices in a mesh: dom: 256 (over x, z, y, core).
Axes of the slice: x: 4, y: 4, z: 8, core: 2. Of those that a mesh axis runs over, the one named last changes fastest.
Arguments:
- stress: float32 [6, 786432], P(None, 'dom'), may hold values from -6 to 6
- stress_dir: float32 [6, 786432], P(None, 'dom'), may hold values from -6 to 6
- adjoint: float32 [6, 786432], P(None, 'dom'), may hold values from -6 to 6
- relax: float32 [786432], P('dom'), may hold values from 0.2 to 2
- relax_dir: float32 [786432], P('dom'), may hold values from -6 to 6
- connect: int32 [4, 4194304], P(None, 'dom'), may hold values from 0 to 5119, as said below
- mass_mat: float32 [16, 4194304], P(None, 'dom'), may hold values from 0.02 to 0.1
- adv_mat: float32 [16, 4194304], P(None, 'dom'), may hold values from -0.6 to 0.6
- vel_grad: float32 [9, 4194304], P(None, 'dom'), may hold values from -3 to 3
- send_list: int32 [524288], P('dom'), may hold values from -1 to 3071, as said below
- elem_count: int32 [256], P('dom'), may hold values from 4096 to 16384, as said below
Outputs:
- inc_residual: float32 [6, 786432], P(None, 'dom')
- hess_action: float32 [786432], P('dom')
Inputs may be any that keep to these rules, and one draw needn't show every extreme that they name: `connect`: each device's entries are below 5120; an entry at or above 3072 names a ghost slot that holds a node. In element block b (slots b * 512 to (b + 1) * 512 - 1) an owned entry lies in start_b to start_b + 383 with start_b = (b * 2688) // max(31, 1), and a ghost entry lies in list b % 16. `send_list`: in each list the live entries (owned node indices) come first, the rest are -1; a list to a neighbour off the ends of the axis is all -1; every partition has a list with all 128 slots live. `elem_count`: some partition has all 16384 slots live and another has 4096.
All inputs are finite; a program needn't handle non-finite values.
Results may differ from a plain program's by a relative error of at most 0.0003.
Values sent between devices are 32-bit elements; how exact they have to be, the bound alone decides.
A program may use at most 64 MiB of HBM per device.

v0:
```python
import jax
import jax.numpy as jnp
from jax import lax
from jax.sharding import PartitionSpec as P

HOPS = 8
ELEM_BLOCK = 512


KAPPA = 0.5
PAIRS = ((0, 0), (1, 1), (2, 2), (0, 1), (0, 2), (1, 2))
LAYOUT = ((0, 3, 4), (3, 1, 5), (4, 5, 2))


def passed_along(block, axis, distance):
    devices = range(lax.axis_size(axis))
    route = [(i - distance, i) for i in devices if i - distance in devices]
    return lax.ppermute(block, axis, route)


def full_tensor(comps):
    return [[comps[LAYOUT[row][col]] for col in range(3)] for row in range(3)]


def convect(grad, comps):
    tensor = full_tensor(comps)
    result = []
    for row, col in PAIRS:
        total = jnp.zeros_like(comps[0])
        for inner in range(3):
            total = (
                total
                + grad[3 * row + inner] * tensor[inner][col]
                + tensor[row][inner] * grad[3 * col + inner]
            )
        result.append(total)
    return jnp.stack(result)


def pair_product(first, second):
    left = full_tensor(first)
    right = full_tensor(second)
    result = []
    for row, col in PAIRS:
        total = jnp.zeros_like(first[0])
        for inner in range(3):
            total = (
                total + left[row][inner] * right[inner][col] + right[row][inner] * left[inner][col]
            )
        result.append(total)
    return jnp.stack(result)


def apply_matrix(matrix, field):
    rows_out = []
    for first in range(4):
        total = jnp.zeros_like(field[:, 0])
        for second in range(4):
            total = total + matrix[4 * first + second] * field[:, second]
        rows_out.append(total)
    return jnp.stack(rows_out, axis=1)


def element_terms(values, mass, advect, grad, live):
    tau = values[0:6]
    tdir = values[6:12]
    adj = values[12:18]
    lam_e = jnp.mean(values[18], axis=0)
    dlam_e = jnp.mean(values[19], axis=0)
    gterm = (
        apply_matrix(advect, tdir)
        - apply_matrix(mass, convect(grad, tdir))
        + KAPPA * apply_matrix(mass, pair_product(tau, tdir))
    )
    bterm = (
        apply_matrix(advect, tau)
        - apply_matrix(mass, convect(grad, tau))
        + 0.5 * KAPPA * apply_matrix(mass, pair_product(tau, tau))
    )
    dres = apply_matrix(mass, tdir) + lam_e * gterm + dlam_e * bterm
    score = 0.25 * jnp.sum(adj * gterm, axis=(0, 1))
    hterm = jnp.broadcast_to(score, dres.shape[1:])[None]
    weight = live.astype(jnp.float32)
    return jnp.concatenate([dres, hterm], axis=0) * weight


def direct_route(pieces, offsets, mover):
    return [mover(piece, offset) for piece, offset in zip(pieces, offsets)]


def shards(
    stress,
    stress_dir,
    adjoint,
    relax,
    relax_dir,
    connect,
    mass_mat,
    adv_mat,
    vel_grad,
    send_list,
    elem_count,
):
    node_dev = stress.shape[1]
    elem_dev = connect.shape[1]
    capacity = send_list.shape[0] // (2 * HOPS)
    window = node_dev // 8
    nblocks = elem_dev // ELEM_BLOCK
    span = max(nblocks - 1, 1)
    offsets = list(range(1, HOPS + 1)) + [-value for value in range(1, HOPS + 1)]
    backwards = [-value for value in offsets]
    fields = jnp.concatenate([stress, stress_dir, adjoint, relax[None], relax_dir[None]], axis=0)
    sends = send_list.reshape(2 * HOPS, capacity)
    valid = (sends >= 0).astype(jnp.float32)
    safe = jnp.where(sends >= 0, sends, 0)
    outgoing = fields[:, safe] * valid[None]
    out_pieces = [outgoing[:, index] for index in range(2 * HOPS)]
    arrived = direct_route(
        out_pieces, offsets, lambda data, amount: passed_along(data, "dom", amount)
    )
    ghost_in = jnp.stack(arrived, axis=0)
    count = elem_count[0]
    columns = jnp.arange(window + capacity, dtype=jnp.int32)

    def visit(block, carry):
        own_acc, ghost_acc = carry
        start = block * ELEM_BLOCK
        conn_block = lax.dynamic_slice_in_dim(connect, start, ELEM_BLOCK, 1)
        mass_block = lax.dynamic_slice_in_dim(mass_mat, start, ELEM_BLOCK, 1)
        adv_block = lax.dynamic_slice_in_dim(adv_mat, start, ELEM_BLOCK, 1)
        grad_block = lax.dynamic_slice_in_dim(vel_grad, start, ELEM_BLOCK, 1)
        first = block * (node_dev - window) // span
        region = block % (2 * HOPS)
        table = jnp.concatenate(
            [
                lax.dynamic_slice_in_dim(fields, first, window, 1),
                lax.dynamic_index_in_dim(ghost_in, region, 0, keepdims=False),
            ],
            axis=1,
        )
        column = jnp.where(
            conn_block < node_dev,
            conn_block - first,
            conn_block - node_dev - region * capacity + window,
        )
        onehot = (column[:, :, None] == columns[None, None, :]).astype(jnp.float32)
        values = jnp.einsum("fc,kec->fke", table, onehot, precision=lax.Precision.HIGHEST)
        live = start + jnp.arange(ELEM_BLOCK, dtype=jnp.int32) < count
        terms = element_terms(values, mass_block, adv_block, grad_block, live)
        contrib = jnp.einsum("tke,kec->tc", terms, onehot, precision=lax.Precision.HIGHEST)
        own_part = lax.dynamic_slice_in_dim(own_acc, first, window, 1) + contrib[:, :window]
        own_acc = lax.dynamic_update_slice_in_dim(own_acc, own_part, first, 1)
        ghost_part = (
            lax.dynamic_index_in_dim(ghost_acc, region, 0, keepdims=False) + contrib[:, window:]
        )
        ghost_acc = lax.dynamic_update_index_in_dim(ghost_acc, ghost_part, region, 0)
        return (own_acc, ghost_acc)

    start_carry = (
        jnp.zeros((7, node_dev), jnp.float32),
        jnp.zeros((2 * HOPS, 7, capacity), jnp.float32),
    )
    own_total, ghost_terms = lax.fori_loop(0, nblocks, visit, start_carry)
    back_pieces = [ghost_terms[index] for index in range(2 * HOPS)]
    returned = direct_route(
        back_pieces, backwards, lambda data, amount: passed_along(data, "dom", amount)
    )
    stacked = jnp.stack(returned, axis=1) * valid[None]
    owned = own_total.at[:, safe.reshape(-1)].add(stacked.reshape(7, -1))
    return (owned[0:6], owned[6])


def solution(mesh):
    return jax.shard_map(
        shards,
        mesh=mesh,
        in_specs=(
            P(None, "dom"),
            P(None, "dom"),
            P(None, "dom"),
            P("dom"),
            P("dom"),
            P(None, "dom"),
            P(None, "dom"),
            P(None, "dom"),
            P(None, "dom"),
            P("dom"),
            P("dom"),
        ),
        out_specs=(P(None, "dom"), P("dom")),
        check_vma=False,
    )
```

profile of v0, /device:TPU:6, one launch (start us, length us, event | category | flops | bytes accessed | tf_op | source)
XLA Modules:
  0.0 578.6 jit_solution(263952809160278104)
XLA Ops:
  2.0 3.7 concatenate.23
  6.3 5.5 gather_fusion
  14.1 8.0 %collective-permute-start.15 = (f32[20,128]{1,0:T(8,128)S(1)}, f32[20,128]{1,0:T(8,128)S(1)}, u32[]{:S(2)}, u32[]{:S(2)}) collective-permute-start(f32[20,128]{1,0:T(8,128)S(1)} %get-tuple-element.470), channel_id=1, source_target_pairs={{8,0},{9,1},{10,2},{11,3},{12,4},{13,5},{14,6},{15,7},{16,8},{17,9... | collective-permute-start | bytes 30728 | tf_op jit(solution)/shard_map/ppermute | solution.py:18
  22.1 3.9 collective-permute-start.14
  26.0 3.9 collective-permute-start.13
  30.0 3.1 collective-permute-start.12
  35.1 7.8 %collective-permute-done.1 = f32[20,128]{1,0:T(8,128)S(1)} collective-permute-done((f32[20,128]{1,0:T(8,128)S(1)}, f32[20,128]{1,0:T(8,128)S(1)}, u32[]{:S(2)}, u32[]{:S(2)}) %collective-permute-start.1) | collective-permute-done | bytes 10272 | tf_op jit(solution)/shard_map/ppermute | solution.py:18
  44.8 7.6 %collective-permute-done.2 = f32[20,128]{1,0:T(8,128)S(1)} collective-permute-done((f32[20,128]{1,0:T(8,128)S(1)}, f32[20,128]{1,0:T(8,128)S(1)}, u32[]{:S(2)}, u32[]{:S(2)}) %collective-permute-start.2) | collective-permute-done | bytes 10272 | tf_op jit(solution)/shard_map/ppermute | solution.py:18
  54.3 8.2 %collective-permute-done.3 = f32[20,128]{1,0:T(8,128)S(1)} collective-permute-done((f32[20,128]{1,0:T(8,128)S(1)}, f32[20,128]{1,0:T(8,128)S(1)}, u32[]{:S(2)}, u32[]{:S(2)}) %collective-permute-start.3) | collective-permute-done | bytes 10272 | tf_op jit(solution)/shard_map/ppermute | solution.py:18
  64.4 6.1 %collective-permute-done.4 = f32[20,128]{1,0:T(8,128)S(1)} collective-permute-done((f32[20,128]{1,0:T(8,128)S(1)}, f32[20,128]{1,0:T(8,128)S(1)}, u32[]{:S(2)}, u32[]{:S(2)}) %collective-permute-start.4) | collective-permute-done | bytes 10272 | tf_op jit(solution)/shard_map/ppermute | solution.py:18
  72.4 6.7 %collective-permute-done.5 = f32[20,128]{1,0:T(8,128)S(1)} collective-permute-done((f32[20,128]{1,0:T(8,128)S(1)}, f32[20,128]{1,0:T(8,128)S(1)}, u32[]{:S(2)}, u32[]{:S(2)}) %collective-permute-start.5) | collective-permute-done | bytes 10272 | tf_op jit(solution)/shard_map/ppermute | solution.py:18
  81.0 5.2 collective-permute-done.6
  88.1 5.8 collective-permute-done.7
  99.1 3.6 collective-permute-done.9
  102.8 6.4 %collective-permute-start.10 = (f32[20,128]{1,0:T(8,128)S(1)}, f32[20,128]{1,0:T(8,128)S(1)}, u32[]{:S(2)}, u32[]{:S(2)}) collective-permute-start(f32[20,128]{1,0:T(8,128)S(1)} %get-tuple-element.475), channel_id=1, source_target_pairs={{3,0},{4,1},{5,2},{6,3},{7,4},{8,5},{9,6},{10,7},{11,8},{12,9},{13... | collective-permute-start | bytes 30728 | tf_op jit(solution)/shard_map/ppermute | solution.py:18
  110.6 7.8 %collective-permute-start.11 = (f32[20,128]{1,0:T(8,128)S(1)}, f32[20,128]{1,0:T(8,128)S(1)}, u32[]{:S(2)}, u32[]{:S(2)}) collective-permute-start(f32[20,128]{1,0:T(8,128)S(1)} %get-tuple-element.474), channel_id=1, source_target_pairs={{4,0},{5,1},{6,2},{7,3},{8,4},{9,5},{10,6},{11,7},{12,8},{13,9},{1... | collective-permute-start | bytes 30728 | tf_op jit(solution)/shard_map/ppermute | solution.py:18
  119.9 331.9 %while.18 = (s32[]{:T(128)}, f32[7,3072]{1,0:T(8,128)S(1)}, f32[16,7,128]{2,1,0:T(8,128)S(1)}, f32[16,16384]{1,0:T(8,128)}, f32[20,3072]{1,0:T(8,128)S(1)}, /*in...) while((s32[]{:T(128)}, f32[7,3072]{1,0:T(8,128)S(1)}, ...), condition=%wide.region_4.5_spmd.clone, body=%wide.region_0.4_spmd.clone.sunk | while | flops 343341632 | bytes 3979695 | solution.py:163
  451.8 12.3 %collective-permute-start.16 = (f32[7,128]{1,0:T(8,128)S(1)}, f32[7,128]{1,0:T(8,128)S(1)}, u32[]{:S(2)}, u32[]{:S(2)}) collective-permute-start(f32[7,128]{1,0:T(8,128)S(1)} %get-tuple-element.501), channel_id=1, source_target_pairs={{1,0},{2,1},{3,2},{4,3},{5,4},{6,5},{7,6},{8,7},{9,8},{10,9},{11,1... | collective-permute-start | bytes 10760 | tf_op jit(solution)/shard_map/ppermute | solution.py:18
  474.4 3.6 collective-permute-done.17
  477.9 5.5 collective-permute-start.18
  484.8 4.7 collective-permute-start.19
  489.6 2.2 collective-permute-done.19
  491.8 4.0 collective-permute-start.20
  495.8 2.4 collective-permute-done.20
  498.2 7.0 %collective-permute-start.21 = (f32[7,128]{1,0:T(8,128)S(1)}, f32[7,128]{1,0:T(8,128)S(1)}, u32[]{:S(2)}, u32[]{:S(2)}) collective-permute-start(f32[7,128]{1,0:T(8,128)S(1)} %get-tuple-element.496), channel_id=1, source_target_pairs={{6,0},{7,1},{8,2},{9,3},{10,4},{11,5},{12,6},{13,7},{14,8},{15,9},... | collective-permute-start | bytes 10760 | tf_op jit(solution)/shard_map/ppermute | solution.py:18
  506.5 5.9 %collective-permute-start.22 = (f32[7,128]{1,0:T(8,128)S(1)}, f32[7,128]{1,0:T(8,128)S(1)}, u32[]{:S(2)}, u32[]{:S(2)}) collective-permute-start(f32[7,128]{1,0:T(8,128)S(1)} %get-tuple-element.495), channel_id=1, source_target_pairs={{7,0},{8,1},{9,2},{10,3},{11,4},{12,5},{13,6},{14,7},{15,8},{16,9}... | collective-permute-start | bytes 10760 | tf_op jit(solution)/shard_map/ppermute | solution.py:18
  513.8 9.1 %collective-permute-start.23 = (f32[7,128]{1,0:T(8,128)S(1)}, f32[7,128]{1,0:T(8,128)S(1)}, u32[]{:S(2)}, u32[]{:S(2)}) collective-permute-start(f32[7,128]{1,0:T(8,128)S(1)} %get-tuple-element.494), channel_id=1, source_target_pairs={{8,0},{9,1},{10,2},{11,3},{12,4},{13,5},{14,6},{15,7},{16,8},{17,9... | collective-permute-start | bytes 10760 | tf_op jit(solution)/shard_map/ppermute | solution.py:18
  526.1 7.2 %collective-permute-done.24 = f32[7,128]{1,0:T(8,128)S(1)} collective-permute-done((f32[7,128]{1,0:T(8,128)S(1)}, f32[7,128]{1,0:T(8,128)S(1)}, u32[]{:S(2)}, u32[]{:S(2)}) %collective-permute-start.24) | collective-permute-done | bytes 3616 | tf_op jit(solution)/shard_map/ppermute | solution.py:18
  535.2 8.0 %collective-permute-done.25 = f32[7,128]{1,0:T(8,128)S(1)} collective-permute-done((f32[7,128]{1,0:T(8,128)S(1)}, f32[7,128]{1,0:T(8,128)S(1)}, u32[]{:S(2)}, u32[]{:S(2)}) %collective-permute-start.25) | collective-permute-done | bytes 3616 | tf_op jit(solution)/shard_map/ppermute | solution.py:18
  545.1 7.5 %collective-permute-done.26 = f32[7,128]{1,0:T(8,128)S(1)} collective-permute-done((f32[7,128]{1,0:T(8,128)S(1)}, f32[7,128]{1,0:T(8,128)S(1)}, u32[]{:S(2)}, u32[]{:S(2)}) %collective-permute-start.26) | collective-permute-done | bytes 3616 | tf_op jit(solution)/shard_map/ppermute | solution.py:18
  554.5 8.1 %collective-permute-done.27 = f32[7,128]{1,0:T(8,128)S(1)} collective-permute-done((f32[7,128]{1,0:T(8,128)S(1)}, f32[7,128]{1,0:T(8,128)S(1)}, u32[]{:S(2)}, u32[]{:S(2)}) %collective-permute-start.27) | collective-permute-done | bytes 3616 | tf_op jit(solution)/shard_map/ppermute | solution.py:18
  563.1 12.9 %scatter_fusion = f32[7,3072]{0,1:T(8,128)S(1)} fusion(f32[7,3072]{0,1:T(8,128)S(1)} %copy.59, s32[2048]{0:T(1024)S(1)} %get-tuple-element.504, f32[2048,7]{1,0:T(8,128)S(1)} %copy.60), kind=kCustom, calls=%fused_computation.1 | custom fusion | flops 14336 | bytes 180224 | tf_op jit(solution)/shard_map/scatter-add | solution.py:169
  (1650 shorter events, 374.4 us)
Async XLA Ops:
  12.1 20.9 %collective-permute-start = (f32[20,128]{1,0:T(8,128)S(1)}, f32[20,128]{1,0:T(8,128)S(1)}, u32[]{:S(2)}, u32[]{:S(2)}) collective-permute-start(f32[20,128]{1,0:T(8,128)S(1)} %get-tuple-element.485), channel_id=1, source_target_pairs={{0,1},{1,2},{2,3},{3,4},{4,5},{5,6},{6,7},{7,8},{8,9},{9,10},{10,1... | collective-permute-start | bytes 30728 | tf_op jit(solution)/shard_map/ppermute | solution.py:18
  14.1 105.8 %collective-permute-start.15 = (f32[20,128]{1,0:T(8,128)S(1)}, f32[20,128]{1,0:T(8,128)S(1)}, u32[]{:S(2)}, u32[]{:S(2)}) collective-permute-start(f32[20,128]{1,0:T(8,128)S(1)} %get-tuple-element.470), channel_id=1, source_target_pairs={{8,0},{9,1},{10,2},{11,3},{12,4},{13,5},{14,6},{15,7},{16,8},{17,9... | collective-permute-start | bytes 30728 | tf_op jit(solution)/shard_map/ppermute | solution.py:18
  22.1 97.7 %collective-permute-start.14 = (f32[20,128]{1,0:T(8,128)S(1)}, f32[20,128]{1,0:T(8,128)S(1)}, u32[]{:S(2)}, u32[]{:S(2)}) collective-permute-start(f32[20,128]{1,0:T(8,128)S(1)} %get-tuple-element.471), channel_id=1, source_target_pairs={{7,0},{8,1},{9,2},{10,3},{11,4},{12,5},{13,6},{14,7},{15,8},{16,9}... | collective-permute-start | bytes 30728 | tf_op jit(solution)/shard_map/ppermute | solution.py:18
  26.0 93.8 %collective-permute-start.13 = (f32[20,128]{1,0:T(8,128)S(1)}, f32[20,128]{1,0:T(8,128)S(1)}, u32[]{:S(2)}, u32[]{:S(2)}) collective-permute-start(f32[20,128]{1,0:T(8,128)S(1)} %get-tuple-element.472), channel_id=1, source_target_pairs={{6,0},{7,1},{8,2},{9,3},{10,4},{11,5},{12,6},{13,7},{14,8},{15,9},... | collective-permute-start | bytes 30728 | tf_op jit(solution)/shard_map/ppermute | solution.py:18
  30.0 89.8 %collective-permute-start.12 = (f32[20,128]{1,0:T(8,128)S(1)}, f32[20,128]{1,0:T(8,128)S(1)}, u32[]{:S(2)}, u32[]{:S(2)}) collective-permute-start(f32[20,128]{1,0:T(8,128)S(1)} %get-tuple-element.473), channel_id=1, source_target_pairs={{5,0},{6,1},{7,2},{8,3},{9,4},{10,5},{11,6},{12,7},{13,8},{14,9},{... | collective-permute-start | bytes 30728 | tf_op jit(solution)/shard_map/ppermute | solution.py:18
  33.1 9.8 %collective-permute-start.1 = (f32[20,128]{1,0:T(8,128)S(1)}, f32[20,128]{1,0:T(8,128)S(1)}, u32[]{:S(2)}, u32[]{:S(2)}) collective-permute-start(f32[20,128]{1,0:T(8,128)S(1)} %get-tuple-element.484), channel_id=1, source_target_pairs={{0,2},{1,3},{2,4},{3,5},{4,6},{5,7},{6,8},{7,9},{8,10},{9,11},{10,... | collective-permute-start | bytes 30728 | tf_op jit(solution)/shard_map/ppermute | solution.py:18
  42.9 9.5 %collective-permute-start.2 = (f32[20,128]{1,0:T(8,128)S(1)}, f32[20,128]{1,0:T(8,128)S(1)}, u32[]{:S(2)}, u32[]{:S(2)}) collective-permute-start(f32[20,128]{1,0:T(8,128)S(1)} %get-tuple-element.483), channel_id=1, source_target_pairs={{0,3},{1,4},{2,5},{3,6},{4,7},{5,8},{6,9},{7,10},{8,11},{9,12},{10... | collective-permute-start | bytes 30728 | tf_op jit(solution)/shard_map/ppermute | solution.py:18
  52.4 10.1 %collective-permute-start.3 = (f32[20,128]{1,0:T(8,128)S(1)}, f32[20,128]{1,0:T(8,128)S(1)}, u32[]{:S(2)}, u32[]{:S(2)}) collective-permute-start(f32[20,128]{1,0:T(8,128)S(1)} %get-tuple-element.482), channel_id=1, source_target_pairs={{0,4},{1,5},{2,6},{3,7},{4,8},{5,9},{6,10},{7,11},{8,12},{9,13},{1... | collective-permute-start | bytes 30728 | tf_op jit(solution)/shard_map/ppermute | solution.py:18
  62.5 8.0 %collective-permute-start.4 = (f32[20,128]{1,0:T(8,128)S(1)}, f32[20,128]{1,0:T(8,128)S(1)}, u32[]{:S(2)}, u32[]{:S(2)}) collective-permute-start(f32[20,128]{1,0:T(8,128)S(1)} %get-tuple-element.481), channel_id=1, source_target_pairs={{0,5},{1,6},{2,7},{3,8},{4,9},{5,10},{6,11},{7,12},{8,13},{9,14},{... | collective-permute-start | bytes 30728 | tf_op jit(solution)/shard_map/ppermute | solution.py:18
  70.5 8.6 %collective-permute-start.5 = (f32[20,128]{1,0:T(8,128)S(1)}, f32[20,128]{1,0:T(8,128)S(1)}, u32[]{:S(2)}, u32[]{:S(2)}) collective-permute-start(f32[20,128]{1,0:T(8,128)S(1)} %get-tuple-element.480), channel_id=1, source_target_pairs={{0,6},{1,7},{2,8},{3,9},{4,10},{5,11},{6,12},{7,13},{8,14},{9,15},... | collective-permute-start | bytes 30728 | tf_op jit(solution)/shard_map/ppermute | solution.py:18
  79.1 7.1 %collective-permute-start.6 = (f32[20,128]{1,0:T(8,128)S(1)}, f32[20,128]{1,0:T(8,128)S(1)}, u32[]{:S(2)}, u32[]{:S(2)}) collective-permute-start(f32[20,128]{1,0:T(8,128)S(1)} %get-tuple-element.479), channel_id=1, source_target_pairs={{0,7},{1,8},{2,9},{3,10},{4,11},{5,12},{6,13},{7,14},{8,15},{9,16}... | collective-permute-start | bytes 30728 | tf_op jit(solution)/shard_map/ppermute | solution.py:18
  86.2 7.7 %collective-permute-start.7 = (f32[20,128]{1,0:T(8,128)S(1)}, f32[20,128]{1,0:T(8,128)S(1)}, u32[]{:S(2)}, u32[]{:S(2)}) collective-permute-start(f32[20,128]{1,0:T(8,128)S(1)} %get-tuple-element.478), channel_id=1, source_target_pairs={{0,8},{1,9},{2,10},{3,11},{4,12},{5,13},{6,14},{7,15},{8,16},{9,17... | collective-permute-start | bytes 30728 | tf_op jit(solution)/shard_map/ppermute | solution.py:18
  93.9 3.3 collective-permute-start.8
  97.2 5.6 collective-permute-start.9
  102.8 7.8 %collective-permute-start.10 = (f32[20,128]{1,0:T(8,128)S(1)}, f32[20,128]{1,0:T(8,128)S(1)}, u32[]{:S(2)}, u32[]{:S(2)}) collective-permute-start(f32[20,128]{1,0:T(8,128)S(1)} %get-tuple-element.475), channel_id=1, source_target_pairs={{3,0},{4,1},{5,2},{6,3},{7,4},{8,5},{9,6},{10,7},{11,8},{12,9},{13... | collective-permute-start | bytes 30728 | tf_op jit(solution)/shard_map/ppermute | solution.py:18
  110.6 9.2 %collective-permute-start.11 = (f32[20,128]{1,0:T(8,128)S(1)}, f32[20,128]{1,0:T(8,128)S(1)}, u32[]{:S(2)}, u32[]{:S(2)}) collective-permute-start(f32[20,128]{1,0:T(8,128)S(1)} %get-tuple-element.474), channel_id=1, source_target_pairs={{4,0},{5,1},{6,2},{7,3},{8,4},{9,5},{10,6},{11,7},{12,8},{13,9},{1... | collective-permute-start | bytes 30728 | tf_op jit(solution)/shard_map/ppermute | solution.py:18
  451.8 20.6 %collective-permute-start.16 = (f32[7,128]{1,0:T(8,128)S(1)}, f32[7,128]{1,0:T(8,128)S(1)}, u32[]{:S(2)}, u32[]{:S(2)}) collective-permute-start(f32[7,128]{1,0:T(8,128)S(1)} %get-tuple-element.501), channel_id=1, source_target_pairs={{1,0},{2,1},{3,2},{4,3},{5,4},{6,5},{7,6},{8,7},{9,8},{10,9},{11,1... | collective-permute-start | bytes 10760 | tf_op jit(solution)/shard_map/ppermute | solution.py:18
  464.2 98.5 %collective-permute-start.31 = (f32[7,128]{1,0:T(8,128)S(1)}, f32[7,128]{1,0:T(8,128)S(1)}, u32[]{:S(2)}, u32[]{:S(2)}) collective-permute-start(f32[7,128]{1,0:T(8,128)S(1)} %get-tuple-element.486), channel_id=1, source_target_pairs={{0,8},{1,9},{2,10},{3,11},{4,12},{5,13},{6,14},{7,15},{8,16},{9,17... | collective-permute-start | bytes 10760 | tf_op jit(solution)/shard_map/ppermute | solution.py:18
  466.1 96.5 %collective-permute-start.30 = (f32[7,128]{1,0:T(8,128)S(1)}, f32[7,128]{1,0:T(8,128)S(1)}, u32[]{:S(2)}, u32[]{:S(2)}) collective-permute-start(f32[7,128]{1,0:T(8,128)S(1)} %get-tuple-element.487), channel_id=1, source_target_pairs={{0,7},{1,8},{2,9},{3,10},{4,11},{5,12},{6,13},{7,14},{8,15},{9,16}... | collective-permute-start | bytes 10760 | tf_op jit(solution)/shard_map/ppermute | solution.py:18
  468.0 94.6 %collective-permute-start.29 = (f32[7,128]{1,0:T(8,128)S(1)}, f32[7,128]{1,0:T(8,128)S(1)}, u32[]{:S(2)}, u32[]{:S(2)}) collective-permute-start(f32[7,128]{1,0:T(8,128)S(1)} %get-tuple-element.488), channel_id=1, source_target_pairs={{0,6},{1,7},{2,8},{3,9},{4,10},{5,11},{6,12},{7,13},{8,14},{9,15},... | collective-permute-start | bytes 10760 | tf_op jit(solution)/shard_map/ppermute | solution.py:18
  470.0 92.7 %collective-permute-start.28 = (f32[7,128]{1,0:T(8,128)S(1)}, f32[7,128]{1,0:T(8,128)S(1)}, u32[]{:S(2)}, u32[]{:S(2)}) collective-permute-start(f32[7,128]{1,0:T(8,128)S(1)} %get-tuple-element.489), channel_id=1, source_target_pairs={{0,5},{1,6},{2,7},{3,8},{4,9},{5,10},{6,11},{7,12},{8,13},{9,14},{... | collective-permute-start | bytes 10760 | tf_op jit(solution)/shard_map/ppermute | solution.py:18
  472.4 5.5 collective-permute-start.17
  477.9 6.9 %collective-permute-start.18 = (f32[7,128]{1,0:T(8,128)S(1)}, f32[7,128]{1,0:T(8,128)S(1)}, u32[]{:S(2)}, u32[]{:S(2)}) collective-permute-start(f32[7,128]{1,0:T(8,128)S(1)} %get-tuple-element.499), channel_id=1, source_target_pairs={{3,0},{4,1},{5,2},{6,3},{7,4},{8,5},{9,6},{10,7},{11,8},{12,9},{13... | collective-permute-start | bytes 10760 | tf_op jit(solution)/shard_map/ppermute | solution.py:18
  484.8 7.0 %collective-permute-start.19 = (f32[7,128]{1,0:T(8,128)S(1)}, f32[7,128]{1,0:T(8,128)S(1)}, u32[]{:S(2)}, u32[]{:S(2)}) collective-permute-start(f32[7,128]{1,0:T(8,128)S(1)} %get-tuple-element.498), channel_id=1, source_target_pairs={{4,0},{5,1},{6,2},{7,3},{8,4},{9,5},{10,6},{11,7},{12,8},{13,9},{1... | collective-permute-start | bytes 10760 | tf_op jit(solution)/shard_map/ppermute | solution.py:18
  491.8 6.4 %collective-permute-start.20 = (f32[7,128]{1,0:T(8,128)S(1)}, f32[7,128]{1,0:T(8,128)S(1)}, u32[]{:S(2)}, u32[]{:S(2)}) collective-permute-start(f32[7,128]{1,0:T(8,128)S(1)} %get-tuple-element.497), channel_id=1, source_target_pairs={{5,0},{6,1},{7,2},{8,3},{9,4},{10,5},{11,6},{12,7},{13,8},{14,9},{... | collective-permute-start | bytes 10760 | tf_op jit(solution)/shard_map/ppermute | solution.py:18
  498.2 8.3 %collective-permute-start.21 = (f32[7,128]{1,0:T(8,128)S(1)}, f32[7,128]{1,0:T(8,128)S(1)}, u32[]{:S(2)}, u32[]{:S(2)}) collective-permute-start(f32[7,128]{1,0:T(8,128)S(1)} %get-tuple-element.496), channel_id=1, source_target_pairs={{6,0},{7,1},{8,2},{9,3},{10,4},{11,5},{12,6},{13,7},{14,8},{15,9},... | collective-permute-start | bytes 10760 | tf_op jit(solution)/shard_map/ppermute | solution.py:18
  506.5 7.2 %collective-permute-start.22 = (f32[7,128]{1,0:T(8,128)S(1)}, f32[7,128]{1,0:T(8,128)S(1)}, u32[]{:S(2)}, u32[]{:S(2)}) collective-permute-start(f32[7,128]{1,0:T(8,128)S(1)} %get-tuple-element.495), channel_id=1, source_target_pairs={{7,0},{8,1},{9,2},{10,3},{11,4},{12,5},{13,6},{14,7},{15,8},{16,9}... | collective-permute-start | bytes 10760 | tf_op jit(solution)/shard_map/ppermute | solution.py:18
  513.8 10.4 %collective-permute-start.23 = (f32[7,128]{1,0:T(8,128)S(1)}, f32[7,128]{1,0:T(8,128)S(1)}, u32[]{:S(2)}, u32[]{:S(2)}) collective-permute-start(f32[7,128]{1,0:T(8,128)S(1)} %get-tuple-element.494), channel_id=1, source_target_pairs={{8,0},{9,1},{10,2},{11,3},{12,4},{13,5},{14,6},{15,7},{16,8},{17,9... | collective-permute-start | bytes 10760 | tf_op jit(solution)/shard_map/ppermute | solution.py:18
  524.2 9.1 %collective-permute-start.24 = (f32[7,128]{1,0:T(8,128)S(1)}, f32[7,128]{1,0:T(8,128)S(1)}, u32[]{:S(2)}, u32[]{:S(2)}) collective-permute-start(f32[7,128]{1,0:T(8,128)S(1)} %get-tuple-element.493), channel_id=1, source_target_pairs={{0,1},{1,2},{2,3},{3,4},{4,5},{5,6},{6,7},{7,8},{8,9},{9,10},{10,1... | collective-permute-start | bytes 10760 | tf_op jit(solution)/shard_map/ppermute | solution.py:18
  533.3 9.9 %collective-permute-start.25 = (f32[7,128]{1,0:T(8,128)S(1)}, f32[7,128]{1,0:T(8,128)S(1)}, u32[]{:S(2)}, u32[]{:S(2)}) collective-permute-start(f32[7,128]{1,0:T(8,128)S(1)} %get-tuple-element.492), channel_id=1, source_target_pairs={{0,2},{1,3},{2,4},{3,5},{4,6},{5,7},{6,8},{7,9},{8,10},{9,11},{10,... | collective-permute-start | bytes 10760 | tf_op jit(solution)/shard_map/ppermute | solution.py:18
  543.2 9.4 %collective-permute-start.26 = (f32[7,128]{1,0:T(8,128)S(1)}, f32[7,128]{1,0:T(8,128)S(1)}, u32[]{:S(2)}, u32[]{:S(2)}) collective-permute-start(f32[7,128]{1,0:T(8,128)S(1)} %get-tuple-element.491), channel_id=1, source_target_pairs={{0,3},{1,4},{2,5},{3,6},{4,7},{5,8},{6,9},{7,10},{8,11},{9,12},{10... | collective-permute-start | bytes 10760 | tf_op jit(solution)/shard_map/ppermute | solution.py:18
  552.6 10.0 %collective-permute-start.27 = (f32[7,128]{1,0:T(8,128)S(1)}, f32[7,128]{1,0:T(8,128)S(1)}, u32[]{:S(2)}, u32[]{:S(2)}) collective-permute-start(f32[7,128]{1,0:T(8,128)S(1)} %get-tuple-element.490), channel_id=1, source_target_pairs={{0,4},{1,5},{2,6},{3,7},{4,8},{5,9},{6,10},{7,11},{8,12},{9,13},{1... | collective-permute-start | bytes 10760 | tf_op jit(solution)/shard_map/ppermute | solution.py:18
where the time goes:
time: 587 us; the launch traced here: 579 us
  local copies, waits for them, and re-layouts  123 us (21%)
  other arithmetic  118 us (20%)
  starting transfers between devices  118 us (20%)
  matrix products  110 us (19%)
  waiting for transfers between devices  99.1 us (17%)
  loops' own time  9.25 us (2%)
    ppermute x32, starting transfers between devices, passed_along(): return lax.ppermute(block, axis, route)  118 us
    ppermute x32, waiting for transfers between devices, passed_along(): return lax.ppermute(block, axis, route)  99.1 us
    slice x96, local copies, waits for them, and re-layouts, apply_matrix(): total = total + matrix[4 * first + second] * field[:, second]  93.7 us
    dot_general x32, matrix products, visit(): jnp.einsum('fc,kec->fke', table, onehot, precision=lax.Precision.HIGHEST)  63.5 us
    dot_general x32, matrix products, visit(): jnp.einsum('tke,kec->tc', terms, onehot, precision=lax.Precision.HIGHEST)  46.5 us
    add x448, other arithmetic, apply_matrix(): total = total + matrix[4 * first + second] * field[:, second]  30.4 us
    select_n x32, other arithmetic, visit(): jnp.where(conn_block < node_dev, conn_block - first, conn_block - node_de...  22.7 us
    convert_element_type x32, other arithmetic, element_terms(): weight = live.astype(jnp.float32)  20.8 us
  transfers between devices with their start and end apart: 32, of which 22 were waited for; matrix products, arithmetic and copies ran while one was open for 0% of the time, Pallas kernels for 0%

commit v1 on v0

v1 whole, which is shorter than its diff:
```python
import jax
import jax.numpy as jnp
from jax import lax
from jax.experimental import pallas as pl
from jax.experimental.pallas import tpu as pltpu
from jax.sharding import PartitionSpec as P

HOPS = 8
LISTS = 2 * HOPS
ELEM_BLOCK = 512
KAPPA = 0.5
PAIRS = ((0, 0), (1, 1), (2, 2), (0, 1), (0, 2), (1, 2))
LAYOUT = ((0, 3, 4), (3, 1, 5), (4, 5, 2))

LANES = 128
ROWS = 24
TAU, LAM, DLAM, DIR, ADJ = 0, 6, 7, 8, 16
FIELD_ROWS = tuple(range(0, 14)) + tuple(range(16, 22))
WIN = 3
TERM = 8

GATHER = lax.GatherDimensionNumbers(
    offset_dims=(),
    collapsed_slice_dims=(1,),
    start_index_map=(1,),
    operand_batching_dims=(0,),
    start_indices_batching_dims=(0,),
)


def pick_lanes(table, lane):
    return lax.gather(
        table,
        lane[:, :, None],
        GATHER,
        slice_sizes=(1, 1),
        mode=lax.GatherScatterMode.PROMISE_IN_BOUNDS,
    )


def list_offset(index):
    return jnp.where(index < HOPS, index + 1, HOPS - 1 - index)


def row_of(ref, row, height=8):
    return jnp.broadcast_to(ref[pl.ds(row, 1), :], (height, LANES))


def two_parts(values):
    high = values.astype(jnp.bfloat16)
    low = (values - high.astype(jnp.float32)).astype(jnp.bfloat16)
    return jnp.concatenate([high, low], axis=0)


def symmetric_product(left, right):
    prod = [
        [
            left[row][0] * right[LAYOUT[0][col]]
            + left[row][1] * right[LAYOUT[1][col]]
            + left[row][2] * right[LAYOUT[2][col]]
            for col in range(3)
        ]
        for row in range(3)
    ]
    return [prod[row][col] + prod[col][row] for row, col in PAIRS]


def make_kernel(ndev, nodes, elems):
    chunks = nodes // LANES
    nblocks = elems // ELEM_BLOCK
    groups = ELEM_BLOCK // LANES
    steps = nblocks // 2
    span = max(nblocks - 1, 1)
    window = WIN * LANES

    def kernel(
        stress_hbm,
        dir_hbm,
        adj_hbm,
        relax_hbm,
        rdir_hbm,
        conn_hbm,
        mass_hbm,
        adv_hbm,
        grad_hbm,
        send_hbm,
        count_ref,
        res_hbm,
        hess_hbm,
        stress,
        sdir,
        adjoint,
        relax,
        rdir,
        conn,
        mass,
        adv,
        grad,
        send,
        res,
        hess,
        fields,
        payload,
        ghosts,
        rolled,
        values,
        gradv,
        grad8,
        index_rows,
        terms,
        acc,
        gout,
        returned,
        in_sem,
        out_sem,
        send_sem,
        recv_sem,
        back_sem,
        ret_sem,
    ):
        me = lax.axis_index("dom")
        loads = [
            pltpu.make_async_copy(src, dst, in_sem.at[i])
            for i, (src, dst) in enumerate(
                [
                    (stress_hbm, stress),
                    (dir_hbm, sdir),
                    (adj_hbm, adjoint),
                    (relax_hbm, relax),
                    (rdir_hbm, rdir),
                    (send_hbm, send),
                    (conn_hbm, conn),
                    (grad_hbm, grad),
                    (mass_hbm, mass),
                    (adv_hbm, adv),
                ]
            )
        ]
        for load in loads:
            load.start()

        def inside(device):
            return (device >= 0) & (device < ndev)

        barrier = pltpu.get_barrier_semaphore()

        @pl.loop(0, LISTS)
        def _(k):
            target = me + list_offset(k)

            @pl.when(inside(target))
            def _():
                pl.semaphore_signal(
                    barrier, inc=1, device_id=(target,), device_id_type=pl.DeviceIdType.MESH
                )

        zeros = jnp.zeros((8, LANES), jnp.float32)
        lane = lax.broadcasted_iota(jnp.int32, (8, LANES), 1)
        sub = lax.broadcasted_iota(jnp.int32, (8, LANES), 0)
        upper = sub >= groups

        for load in loads[:6]:
            load.wait()

        for c in range(chunks):
            cut = pl.ds(c * LANES, LANES)
            for base in (TAU, DIR, ADJ):
                fields[pl.ds(c * ROWS + base, 8), :] = zeros
            fields[pl.ds(c * ROWS + TAU, 6), :] = stress[:, cut]
            fields[pl.ds(c * ROWS + LAM, 1), :] = relax[pl.ds(c, 1), :]
            fields[pl.ds(c * ROWS + DLAM, 1), :] = rdir[pl.ds(c, 1), :]
            fields[pl.ds(c * ROWS + DIR, 6), :] = sdir[:, cut]
            fields[pl.ds(c * ROWS + ADJ, 6), :] = adjoint[:, cut]
        for base in (TAU, DIR, ADJ):
            fields[pl.ds(chunks * ROWS + base, 8), :] = zeros

        @pl.loop(0, LISTS)
        def _(k):
            entry = row_of(send, k)
            place = entry & (LANES - 1)
            chunk = entry >> 7
            picked = [zeros, zeros, zeros]
            for c in range(chunks):
                here = chunk == c
                for t in range(3):
                    got = pick_lanes(fields[pl.ds(c * ROWS + 8 * t, 8), :], place)
                    picked[t] = jnp.where(here, got, picked[t])
            for t in range(3):
                payload[k, pl.ds(8 * t, 8), :] = picked[t]

        first_up = jnp.minimum(HOPS, ndev - 1 - me)
        first_down = jnp.minimum(HOPS, me)
        pl.semaphore_wait(barrier, first_up + first_down)

        def push(k):
            target = me + list_offset(k)
            return pltpu.make_async_remote_copy(
                src_ref=payload.at[k],
                dst_ref=ghosts.at[k],
                send_sem=send_sem.at[k],
                recv_sem=recv_sem.at[k],
                device_id=(target,),
                device_id_type=pl.DeviceIdType.MESH,
            )

        def push_back(k):
            target = me - list_offset(k)
            return pltpu.make_async_remote_copy(
                src_ref=gout.at[k],
                dst_ref=returned.at[k],
                send_sem=back_sem.at[k],
                recv_sem=ret_sem.at[k],
                device_id=(target,),
                device_id_type=pl.DeviceIdType.MESH,
            )

        @pl.loop(0, LISTS)
        def _(k):
            @pl.when(inside(me + list_offset(k)))
            def _():
                push(k).start()

        for i in range(chunks + 1):
            acc[pl.ds(i * TERM, TERM), :] = zeros
        for i in range(LISTS):
            gout[i] = zeros
        for k in range(4):
            for g in range(8):
                terms[k, pl.ds(g * TERM, TERM), :] = zeros

        for load in loads[6:8]:
            load.wait()

        def starts_of(pair):
            one = (2 * pair) * (nodes - window) // span
            two = (2 * pair + 1) * (nodes - window) // span
            return one, two

        def relative(pair, k):
            one, two = starts_of(pair)
            lists_one = (2 * pair) % LISTS
            node = conn[pl.ds(pair * 32 + k, 8, stride=4), :]
            start = jnp.where(upper, two, one)
            ghost0 = nodes + LANES * jnp.where(upper, lists_one + 1, lists_one) - window
            return node - jnp.where(node >= nodes, ghost0, start)

        @pl.loop(0, steps)
        def _(pair):
            for which, start in enumerate(starts_of(pair)):
                chunk0 = start // LANES
                shift = start % LANES
                keep = lane < LANES - shift
                for t in range(3):
                    turned = [
                        pltpu.roll(
                            fields[
                                pl.ds(pl.multiple_of((chunk0 + i) * ROWS + 8 * t, 8), 8), :
                            ],
                            (LANES - shift) % LANES,
                            1,
                        )
                        for i in range(WIN + 1)
                    ]
                    for i in range(WIN):
                        rolled[which, pl.ds(i * ROWS + 8 * t, 8), :] = jnp.where(
                            keep, turned[i], turned[i + 1]
                        )
            places, firsts, seconds = [], [], []
            for k in range(4):
                rel = relative(pair, k)
                places.append(rel & (LANES - 1))
                firsts.append(rel < LANES)
                seconds.append(rel < 2 * LANES)
            for n, row in enumerate(FIELD_ROWS):
                table = [
                    jnp.where(
                        upper,
                        row_of(rolled.at[1], i * ROWS + row),
                        row_of(rolled.at[0], i * ROWS + row),
                    )
                    for i in range(WIN)
                ]
                for k in range(4):
                    a, b, c = [pick_lanes(table[i], places[k]) for i in range(WIN)]
                    values[pair, k * 20 + n] = jnp.where(
                        firsts[k], a, jnp.where(seconds[k], b, c)
                    )
            for j in range(8):
                cut = pl.ds(pl.multiple_of((pair * 8 + j) * LANES, LANES), LANES)
                gradv[pl.ds(pl.multiple_of((pair * 8 + j) * 8, 8), 8), :] = grad[0:8, cut]
                grad8[pl.ds(pair * 8 + j, 1), :] = grad[8:9, cut]

        for load in loads[8:]:
            load.wait()

        count = count_ref[0]
        columns = lax.broadcasted_iota(jnp.int32, (LANES, LANES), 0).astype(jnp.bfloat16)
        one16 = jnp.ones((LANES, LANES), jnp.bfloat16)
        zero16 = jnp.zeros((LANES, LANES), jnp.bfloat16)
        contract = (((1,), (1,)), ((), ()))

        def factor(place_row):
            return jnp.where(columns == place_row, one16, zero16)

        def visit(pair):
            listed = (2 * pair) % LISTS
            rels = [relative(pair, k) for k in range(4)]
            places = [rel & (LANES - 1) for rel in rels]
            ghostly = [rel >= window for rel in rels]
            got = [[None] * 20 for _ in range(4)]
            for n, row in enumerate(FIELD_ROWS):
                table = jnp.where(
                    upper, row_of(ghosts.at[listed + 1], row), row_of(ghosts.at[listed], row)
                )
                for k in range(4):
                    got[k][n] = jnp.where(
                        ghostly[k], pick_lanes(table, places[k]), values[pair, k * 20 + n]
                    )
            lam_e = 0.25 * (got[0][6] + got[1][6] + got[2][6] + got[3][6])
            dlam_e = 0.25 * (got[0][7] + got[1][7] + got[2][7] + got[3][7])
            vel = [
                gradv[pl.ds(pair * 64 + i, 8, stride=8), :] for i in range(8)
            ] + [grad8[pl.ds(pl.multiple_of(pair * 8, 8), 8), :]]
            tdir, gin, wsum, usum = [], [], [], []
            for k in range(4):
                tau = got[k][0:6]
                t = got[k][8:14]
                half = [KAPPA * s for s in tau]
                quarter = [0.5 * s for s in half]
                left_g = [
                    [half[LAYOUT[r][c]] - vel[3 * r + c] for c in range(3)] for r in range(3)
                ]
                left_b = [
                    [quarter[LAYOUT[r][c]] - vel[3 * r + c] for c in range(3)] for r in range(3)
                ]
                b_in = symmetric_product(left_b, tau)
                tdir.append(t)
                gin.append(symmetric_product(left_g, t))
                wsum.append([dlam_e * s for s in tau])
                usum.append([t[c] + dlam_e * b_in[c] for c in range(6)])
            score = zeros
            for a in range(4):
                mat = [
                    mass[pl.ds(((4 * a + b) // 8) * elems // 16 + pair * 64 + (4 * a + b) % 8, 8, stride=8), :]
                    for b in range(4)
                ]
                adm = [
                    adv[pl.ds(((4 * a + b) // 8) * elems // 16 + pair * 64 + (4 * a + b) % 8, 8, stride=8), :]
                    for b in range(4)
                ]
                for c in range(6):
                    g = adm[0] * tdir[0][c] + mat[0] * gin[0][c]
                    d = adm[0] * wsum[0][c] + mat[0] * usum[0][c]
                    for b in range(1, 4):
                        g = g + (adm[b] * tdir[b][c] + mat[b] * gin[b][c])
                        d = d + (adm[b] * wsum[b][c] + mat[b] * usum[b][c])
                    score = score + got[a][14 + c] * g
                    terms[a, pl.ds(c, 8, stride=TERM), :] = d + lam_e * g
            score = 0.25 * score
            for a in range(4):
                terms[a, pl.ds(6, 8, stride=TERM), :] = score

            live = (pair * 8 + sub) * LANES + lane < count
            for k in range(4):
                index_rows[0, pl.ds(8 * k, 8), :] = places[k].astype(jnp.float32)
                index_rows[1, pl.ds(8 * k, 8), :] = jnp.where(live, rels[k] >> 7, -1).astype(
                    jnp.float32
                )
            for which, start in enumerate(starts_of(pair)):
                total = jnp.zeros((4 * 2 * TERM, LANES), jnp.float32)
                for k in range(4):
                    lefts, rights = [], []
                    for j in range(groups):
                        g = which * groups + j
                        part = two_parts(terms[k, pl.ds(g * TERM, TERM), :])
                        chunk = row_of(index_rows.at[1], 8 * k + g, 16).astype(jnp.bfloat16)
                        place = row_of(index_rows.at[0], 8 * k + g, 16).astype(jnp.bfloat16)
                        lefts.append(
                            jnp.concatenate(
                                [
                                    jnp.where(chunk == float(i), part, zero16[:16])
                                    for i in range(4)
                                ],
                                axis=0,
                            )
                        )
                        rights.append(factor(jnp.concatenate([place] * 8, axis=0)))
                    total = total + lax.dot_general(
                        jnp.concatenate(lefts, axis=1),
                        jnp.concatenate(rights, axis=1),
                        contract,
                        preferred_element_type=jnp.float32,
                    )
                sums = [
                    total[16 * i : 16 * i + 8] + total[16 * i + 8 : 16 * i + 16]
                    for i in range(4)
                ]
                chunk0 = start // LANES
                shift = start % LANES
                turned = [pltpu.roll(sums[i], shift, 1) for i in range(WIN)]
                later = lane >= shift
                for i in range(WIN + 1):
                    if i == 0:
                        add = jnp.where(later, turned[0], 0.0)
                    elif i == WIN:
                        add = jnp.where(later, 0.0, turned[WIN - 1])
                    else:
                        add = jnp.where(later, turned[i], turned[i - 1])
                    at = pl.ds(pl.multiple_of((chunk0 + i) * TERM, TERM), TERM)
                    acc[at, :] = acc[at, :] + add
                gout[listed + which] = gout[listed + which] + sums[WIN]

        turns = LISTS // 2
        rounds = steps // turns

        @pl.loop(0, turns)
        def _(turn):
            for which in range(2):
                k = 2 * turn + which

                @pl.when(inside(me - list_offset(k)))
                def _():
                    push(k).wait_recv()

            @pl.loop(0, rounds)
            def _(r):
                visit(turn + r * turns)

            for which in range(2):
                k = 2 * turn + which

                @pl.when(inside(me - list_offset(k)))
                def _():
                    push_back(k).start()

        @pl.loop(0, LISTS)
        def _(k):
            @pl.when(inside(me + list_offset(k)))
            def _():
                push_back(k).wait_recv()

        total = jnp.zeros((chunks * 2 * TERM, LANES), jnp.float32)
        for pairing in range(LISTS // 2):
            lefts, rights = [], []
            for k in (2 * pairing, 2 * pairing + 1):
                entry = row_of(send, k)
                part = two_parts(jnp.where(entry >= 0, returned[k], 0.0))
                entry16 = row_of(send, k, 16)
                chunk = (entry16 >> 7).astype(jnp.float32).astype(jnp.bfloat16)
                place = (entry16 & (LANES - 1)).astype(jnp.float32).astype(jnp.bfloat16)
                lefts.append(
                    jnp.concatenate(
                        [
                            jnp.where(chunk == float(i), part, zero16[:16])
                            for i in range(chunks)
                        ],
                        axis=0,
                    )
                )
                rights.append(factor(jnp.concatenate([place] * 8, axis=0)))
            total = total + lax.dot_general(
                jnp.concatenate(lefts, axis=1),
                jnp.concatenate(rights, axis=1),
                contract,
                preferred_element_type=jnp.float32,
            )
        for c in range(chunks):
            out = (
                acc[pl.ds(c * TERM, TERM), :]
                + total[16 * c : 16 * c + 8]
                + total[16 * c + 8 : 16 * c + 16]
            )
            res[:, pl.ds(c * LANES, LANES)] = out[0:6]
            hess[pl.ds(c, 1), :] = out[6:7]

        stores = [
            pltpu.make_async_copy(res, res_hbm, out_sem.at[0]),
            pltpu.make_async_copy(hess, hess_hbm, out_sem.at[1]),
        ]
        for store in stores:
            store.start()

        @pl.loop(0, LISTS)
        def _(k):
            @pl.when(inside(me + list_offset(k)))
            def _():
                push(k).wait_send()

            @pl.when(inside(me - list_offset(k)))
            def _():
                push_back(k).wait_send()

        for store in stores:
            store.wait()

    return kernel


def shards(
    ndev,
    stress,
    stress_dir,
    adjoint,
    relax,
    relax_dir,
    connect,
    mass_mat,
    adv_mat,
    vel_grad,
    send_list,
    elem_count,
):
    nodes = stress.shape[1]
    elems = connect.shape[1]
    chunks = nodes // LANES
    steps = elems // ELEM_BLOCK // 2
    f32, i32 = jnp.float32, jnp.int32

    def by_groups(matrix, rows):
        split = matrix.reshape(-1, rows, elems // LANES, LANES)
        return split.transpose(0, 2, 1, 3).reshape(-1, LANES)

    args = (
        stress,
        stress_dir,
        adjoint,
        relax.reshape(chunks, LANES),
        relax_dir.reshape(chunks, LANES),
        by_groups(connect, 4),
        by_groups(mass_mat, 8),
        by_groups(adv_mat, 8),
        vel_grad,
        send_list.reshape(LISTS, LANES),
        elem_count,
    )
    hbm = pl.BlockSpec(memory_space=pl.ANY)
    res, hess = pl.pallas_call(
        make_kernel(ndev, nodes, elems),
        out_shape=(
            jax.ShapeDtypeStruct((6, nodes), f32),
            jax.ShapeDtypeStruct((chunks, LANES), f32),
        ),
        in_specs=[hbm] * 10 + [pl.BlockSpec(memory_space=pltpu.SMEM)],
        out_specs=(hbm, hbm),
        scratch_shapes=[
            pltpu.VMEM((6, nodes), f32),
            pltpu.VMEM((6, nodes), f32),
            pltpu.VMEM((6, nodes), f32),
            pltpu.VMEM((chunks, LANES), f32),
            pltpu.VMEM((chunks, LANES), f32),
            pltpu.VMEM((elems // 32, LANES), i32),
            pltpu.VMEM((elems // 8, LANES), f32),
            pltpu.VMEM((elems // 8, LANES), f32),
            pltpu.VMEM((9, elems), f32),
            pltpu.VMEM((LISTS, LANES), i32),
            pltpu.VMEM((6, nodes), f32),
            pltpu.VMEM((chunks, LANES), f32),
            pltpu.VMEM(((chunks + 1) * ROWS, LANES), f32),
            pltpu.VMEM((LISTS, ROWS, LANES), f32),
            pltpu.VMEM((LISTS, ROWS, LANES), f32),
            pltpu.VMEM((2, WIN * ROWS, LANES), f32),
            pltpu.VMEM((steps, 80, 8, LANES), f32),
            pltpu.VMEM((elems // 16, LANES), f32),
            pltpu.VMEM((elems // LANES, LANES), f32),
            pltpu.VMEM((2, 32, LANES), f32),
            pltpu.VMEM((4, 8 * TERM, LANES), f32),
            pltpu.VMEM(((chunks + 1) * TERM, LANES), f32),
            pltpu.VMEM((LISTS, TERM, LANES), f32),
            pltpu.VMEM((LISTS, TERM, LANES), f32),
            pltpu.SemaphoreType.DMA((10,)),
            pltpu.SemaphoreType.DMA((2,)),
            pltpu.SemaphoreType.DMA((LISTS,)),
            pltpu.SemaphoreType.DMA((LISTS,)),
            pltpu.SemaphoreType.DMA((LISTS,)),
            pltpu.SemaphoreType.DMA((LISTS,)),
        ],
        compiler_params=pltpu.CompilerParams(
            collective_id=0,
            has_side_effects=True,
            vmem_limit_bytes=48 * 1024 * 1024,
        ),
    )(*args)
    return res, hess.reshape(nodes)


def solution(mesh):
    ndev = mesh.shape["dom"]

    def run(*args):
        return shards(ndev, *args)

    return jax.shard_map(
        run,
        mesh=mesh,
        in_specs=(
            P(None, "dom"),
            P(None, "dom"),
            P(None, "dom"),
            P("dom"),
            P("dom"),
            P(None, "dom"),
            P(None, "dom"),
            P(None, "dom"),
            P(None, "dom"),
            P("dom"),
            P("dom"),
        ),
        out_specs=(P(None, "dom"), P("dom")),
        check_vma=False,
    )
```

time: 587 us -> 50.7 us (0.09); the launches traced: 579 us -> 50.1 us
  other arithmetic: 118 us -> 0 us
  starting transfers between devices: 118 us -> 0 us
  local copies, waits for them, and re-layouts: 123 us -> 9.99 us
  matrix products: 110 us -> 0 us
  waiting for transfers between devices: 99.1 us -> 0 us
  Pallas kernels: 0 us -> 38.8 us
  loops' own time: 9.25 us -> 0 us
    ppermute x32 -> x0, starting transfers between devices: 118 us -> none  [passed_along(): return lax.ppermute(block, axis, route)]
    dot_general x64 -> x0, matrix products: 110 us -> none  [the longest x32 63.5 us: visit(): jnp.einsum('fc,kec->fke', table, onehot, precision=lax.Precision.HIGHEST)]
    ppermute x32 -> x0, waiting for transfers between devices: 99.1 us -> none  [passed_along(): return lax.ppermute(block, axis, route)]
    slice x129 -> x0, local copies, waits for them, and re-layouts: 95.9 us -> none  [the longest x96 93.7 us: apply_matrix(): total = total + matrix[4 * first + second] * field[:, second]]
    add x512 -> x0, other arithmetic: 44.2 us -> none  [the longest x448 30.4 us: apply_matrix(): total = total + matrix[4 * first + second] * field[:, second]]
    pallas_call x0 -> x1, Pallas kernels: none -> 38.8 us  [shards(): pl.pallas_call(make_kernel(ndev, nodes, elems), out_shape=(jax.ShapeDtype...]
    select_n x33 -> x0, other arithmetic: 23.4 us -> none  [the longest x32 22.7 us: visit(): jnp.where(conn_block < node_dev, conn_block - first, conn_block - node_de...]
    convert_element_type x33 -> x0, other arithmetic: 21.5 us -> none  [the longest x32 20.8 us: element_terms(): weight = live.astype(jnp.float32)]
  transfers between devices with their start and end apart: 32 -> 0, of which waited for: 22 -> 0; matrix products, arithmetic and copies ran while one was open for 0% -> 0% of each run, Pallas kernels for 0% -> 0%
where the time goes in v1:
time: 50.7 us; the launch traced here: 50.1 us
  Pallas kernels  38.8 us (77%)
  local copies, waits for them, and re-layouts  9.99 us (20%)
  between operations  1.32 us (3%)
    pallas_call x1, Pallas kernels, shards(): pl.pallas_call(make_kernel(ndev, nodes, elems), out_shape=(jax.ShapeDtype...  38.8 us
    unnamed x22, local copies, waits for them, and re-layouts  9.99 us

profile of v1, /device:TPU:6, one launch (start us, length us, event | category | flops | bytes accessed | tf_op | source)
XLA Modules:
  0.0 50.1 jit_solution(4294883248365108898)
XLA Ops:
  0.6 0.0 copy-start.7
  1.3 0.0 copy-done.7
  1.3 0.0 copy-start
  1.3 1.2 %copy-done = f32[16,16384]{1,0:T(8,128)S(1)} copy-done((f32[16,16384]{1,0:T(8,128)S(1)}, f32[16,16384]{1,0:T(8,128)}, u32[]{:S(2)}) %copy-start) | copy-done | bytes 1048600
  2.6 0.0 copy-start.1
  2.6 1.2 %copy-done.1 = f32[16,16384]{1,0:T(8,128)S(1)} copy-done((f32[16,16384]{1,0:T(8,128)S(1)}, f32[16,16384]{1,0:T(8,128)}, u32[]{:S(2)}) %copy-start.1) | copy-done | bytes 1048600
  3.8 0.0 copy-start.2
  3.8 1.2 %copy-done.2 = f32[9,16384]{1,0:T(8,128)S(1)} copy-done((f32[9,16384]{1,0:T(8,128)S(1)}, f32[9,16384]{1,0:T(8,128)}, u32[]{:S(2)}) %copy-start.2) | copy-done | bytes 589848
  5.0 0.0 copy-start.3
  5.0 0.9 %copy-done.3 = s32[4,16384]{1,0:T(4,128)S(1)} copy-done((s32[4,16384]{1,0:T(4,128)S(1)}, s32[4,16384]{1,0:T(4,128)}, u32[]{:S(2)}) %copy-start.3) | copy-done | bytes 262168
  6.0 0.0 copy-start.4
  6.0 0.9 %copy-done.4 = f32[6,3072]{1,0:T(8,128)S(1)} copy-done((f32[6,3072]{1,0:T(8,128)S(1)}, f32[6,3072]{1,0:T(8,128)}, u32[]{:S(2)}) %copy-start.4) | copy-done | bytes 73752
  6.9 0.0 copy-start.5
  6.9 0.9 %copy-done.5 = f32[6,3072]{1,0:T(8,128)S(1)} copy-done((f32[6,3072]{1,0:T(8,128)S(1)}, f32[6,3072]{1,0:T(8,128)}, u32[]{:S(2)}) %copy-start.5) | copy-done | bytes 73752
  7.8 0.0 copy-start.6
  7.8 0.9 %copy-done.6 = f32[6,3072]{1,0:T(8,128)S(1)} copy-done((f32[6,3072]{1,0:T(8,128)S(1)}, f32[6,3072]{1,0:T(8,128)}, u32[]{:S(2)}) %copy-start.6) | copy-done | bytes 73752
  8.6 0.0 copy-start.8
  8.7 0.7 %copy-done.8 = f32[3072]{0:T(1024)S(1)} copy-done((f32[3072]{0:T(1024)S(1)}, f32[3072]{0:T(1024)}, u32[]{:S(2)}) %copy-start.8) | copy-done | bytes 12312
  9.4 0.0 copy-start.9
  9.4 0.7 %copy-done.9 = s32[2048]{0:T(1024)S(1)} copy-done((s32[2048]{0:T(1024)S(1)}, s32[2048]{0:T(1024)}, u32[]{:S(2)}) %copy-start.9) | copy-done | bytes 8216
  10.1 38.8 %shard_map.122 = (f32[6,3072]{1,0:T(8,128)S(1)}, f32[24,128]{1,0:T(8,128)S(1)}) custom-call(f32[6,3072]{1,0:T(8,128)S(1)} %copy-done.4, f32[6,3072]{1,0:T(8,128)S(1)} %copy-done.5, f32[6,3072]{1,0:T(8,128)S(1)} %copy-done.6, f32[24,128]{1,0:T(8,128)S(1)} %bitcast.23, f32[24,128]{1,0:T(8,128)S(1)} %bitcast.24, s32[512,128]{1,0:T(8,128)S(1)} %bitcast.21, ...), custom_call_target="tpu_custom_call" | custom-call | tf_op jit(solution)/shard_map/pallas_call | solution.py:537
  48.8 0.6 %copy.17 = f32[6,3072]{1,0:T(8,128)} copy(f32[6,3072]{1,0:T(8,128)S(1)} %get-tuple-element.8) | data formatting | bytes 147456
  49.5 0.6 %copy.18 = f32[3072]{0:T(1024)} copy(f32[3072]{0:T(1024)S(1)} %bitcast.22) | data formatting | bytes 24576
Async XLA Ops:
  0.6 0.7 %copy-start.7 = (f32[3072]{0:T(1024)S(1)}, f32[3072]{0:T(1024)}, u32[]{:S(2)}) copy-start(f32[3072]{0:T(1024)} %param.14) | copy-start | bytes 36868
  1.3 1.2 %copy-start = (f32[16,16384]{1,0:T(8,128)S(1)}, f32[16,16384]{1,0:T(8,128)}, u32[]{:S(2)}) copy-start(f32[16,16384]{1,0:T(8,128)} %param.17) | copy-start | bytes 3145732
  2.6 1.2 %copy-start.1 = (f32[16,16384]{1,0:T(8,128)S(1)}, f32[16,16384]{1,0:T(8,128)}, u32[]{:S(2)}) copy-start(f32[16,16384]{1,0:T(8,128)} %param.18) | copy-start | bytes 3145732
  3.8 1.2 %copy-start.2 = (f32[9,16384]{1,0:T(8,128)S(1)}, f32[9,16384]{1,0:T(8,128)}, u32[]{:S(2)}) copy-start(f32[9,16384]{1,0:T(8,128)} %grad_hbm.1) | copy-start | bytes 1769476
  5.0 0.9 %copy-start.3 = (s32[4,16384]{1,0:T(4,128)S(1)}, s32[4,16384]{1,0:T(4,128)}, u32[]{:S(2)}) copy-start(s32[4,16384]{1,0:T(4,128)} %param.16) | copy-start | bytes 786436
  6.0 0.9 %copy-start.4 = (f32[6,3072]{1,0:T(8,128)S(1)}, f32[6,3072]{1,0:T(8,128)}, u32[]{:S(2)}) copy-start(f32[6,3072]{1,0:T(8,128)} %stress_hbm.1) | copy-start | bytes 221188
  6.9 0.9 %copy-start.5 = (f32[6,3072]{1,0:T(8,128)S(1)}, f32[6,3072]{1,0:T(8,128)}, u32[]{:S(2)}) copy-start(f32[6,3072]{1,0:T(8,128)} %dir_hbm.1) | copy-start | bytes 221188
  7.8 0.9 %copy-start.6 = (f32[6,3072]{1,0:T(8,128)S(1)}, f32[6,3072]{1,0:T(8,128)}, u32[]{:S(2)}) copy-start(f32[6,3072]{1,0:T(8,128)} %adj_hbm.1) | copy-start | bytes 221188
  8.6 0.7 %copy-start.8 = (f32[3072]{0:T(1024)S(1)}, f32[3072]{0:T(1024)}, u32[]{:S(2)}) copy-start(f32[3072]{0:T(1024)} %param.15) | copy-start | bytes 36868
  9.4 0.7 %copy-start.9 = (s32[2048]{0:T(1024)S(1)}, s32[2048]{0:T(1024)}, u32[]{:S(2)}) copy-start(s32[2048]{0:T(1024)} %param.20) | copy-start | bytes 24580

commit v2 on v1

--- a/solution.py
+++ b/solution.py
@@ -102,12 +102,21 @@
         fields,
         payload,
         ghosts,
-        rolled,
+        rolled0,
+        rolled1,
+        table0,
+        table1,
         values,
         gradv,
         grad8,
-        index_rows,
-        terms,
+        gtable0,
+        gtable1,
+        merged0,
+        merged1,
+        index0,
+        index1,
+        terms0,
+        terms1,
         acc,
         gout,
         returned,
@@ -224,9 +233,13 @@
             acc[pl.ds(i * TERM, TERM), :] = zeros
         for i in range(LISTS):
             gout[i] = zeros
+        for terms in (terms0, terms1):
+            for k in range(4):
+                for g in range(8):
+                    terms[k, pl.ds(g * TERM, TERM), :] = zeros
         for k in range(4):
-            for g in range(8):
-                terms[k, pl.ds(g * TERM, TERM), :] = zeros
+            index1[0, pl.ds(8 * k, 8), :] = zeros
+            index1[1, pl.ds(8 * k, 8), :] = zeros - 1.0
 
         for load in loads[6:8]:
             load.wait()
@@ -244,8 +257,7 @@
             ghost0 = nodes + LANES * jnp.where(upper, lists_one + 1, lists_one) - window
             return node - jnp.where(node >= nodes, ghost0, start)
 
-        @pl.loop(0, steps)
-        def _(pair):
+        def prepare(pair, rolled, table):
             for which, start in enumerate(starts_of(pair)):
                 chunk0 = start // LANES
                 shift = start % LANES
@@ -265,30 +277,36 @@
                         rolled[which, pl.ds(i * ROWS + 8 * t, 8), :] = jnp.where(
                             keep, turned[i], turned[i + 1]
                         )
-            places, firsts, seconds = [], [], []
-            for k in range(4):
-                rel = relative(pair, k)
-                places.append(rel & (LANES - 1))
-                firsts.append(rel < LANES)
-                seconds.append(rel < 2 * LANES)
             for n, row in enumerate(FIELD_ROWS):
-                table = [
-                    jnp.where(
+                for i in range(WIN):
+                    table[n * WIN + i] = jnp.where(
                         upper,
                         row_of(rolled.at[1], i * ROWS + row),
                         row_of(rolled.at[0], i * ROWS + row),
                     )
-                    for i in range(WIN)
-                ]
-                for k in range(4):
-                    a, b, c = [pick_lanes(table[i], places[k]) for i in range(WIN)]
-                    values[pair, k * 20 + n] = jnp.where(
-                        firsts[k], a, jnp.where(seconds[k], b, c)
-                    )
+
+        def gather_owned(pair, table):
+            for k in range(4):
+                rel = relative(pair, k)
+                place = rel & (LANES - 1)
+                first = rel < LANES
+                second = rel < 2 * LANES
+                for n in range(20):
+                    a, b, c = [pick_lanes(table[n * WIN + i], place) for i in range(WIN)]
+                    values[pair, k * 20 + n] = jnp.where(first, a, jnp.where(second, b, c))
             for j in range(8):
                 cut = pl.ds(pl.multiple_of((pair * 8 + j) * LANES, LANES), LANES)
                 gradv[pl.ds(pl.multiple_of((pair * 8 + j) * 8, 8), 8), :] = grad[0:8, cut]
                 grad8[pl.ds(pair * 8 + j, 1), :] = grad[8:9, cut]
+
+        prepare(0, rolled0, table0)
+
+        @pl.loop(0, steps // 2)
+        def _(i):
+            gather_owned(2 * i, table0)
+            prepare(2 * i + 1, rolled1, table1)
+            gather_owned(2 * i + 1, table1)
+            prepare(jnp.minimum(2 * i + 2, steps - 1), rolled0, table0)
 
         for load in loads[8:]:
             load.wait()
@@ -302,20 +320,23 @@
         def factor(place_row):
             return jnp.where(columns == place_row, one16, zero16)
 
-        def visit(pair):
+        def gather_ghosts(pair, gtable, merged):
             listed = (2 * pair) % LISTS
-            rels = [relative(pair, k) for k in range(4)]
-            places = [rel & (LANES - 1) for rel in rels]
-            ghostly = [rel >= window for rel in rels]
-            got = [[None] * 20 for _ in range(4)]
             for n, row in enumerate(FIELD_ROWS):
-                table = jnp.where(
+                gtable[n] = jnp.where(
                     upper, row_of(ghosts.at[listed + 1], row), row_of(ghosts.at[listed], row)
                 )
-                for k in range(4):
-                    got[k][n] = jnp.where(
-                        ghostly[k], pick_lanes(table, places[k]), values[pair, k * 20 + n]
+            for k in range(4):
+                rel = relative(pair, k)
+                place = rel & (LANES - 1)
+                ghostly = rel >= window
+                for n in range(20):
+                    merged[k * 20 + n] = jnp.where(
+                        ghostly, pick_lanes(gtable[n], place), values[pair, k * 20 + n]
                     )
+
+        def algebra(pair, merged, terms, index_rows):
+            got = [[merged[k * 20 + n] for n in range(20)] for k in range(4)]
             lam_e = 0.25 * (got[0][6] + got[1][6] + got[2][6] + got[3][6])
             dlam_e = 0.25 * (got[0][7] + got[1][7] + got[2][7] + got[3][7])
             vel = [
@@ -340,14 +361,12 @@
                 usum.append([t[c] + dlam_e * b_in[c] for c in range(6)])
             score = zeros
             for a in range(4):
-                mat = [
-                    mass[pl.ds(((4 * a + b) // 8) * elems // 16 + pair * 64 + (4 * a + b) % 8, 8, stride=8), :]
-                    for b in range(4)
-                ]
-                adm = [
-                    adv[pl.ds(((4 * a + b) // 8) * elems // 16 + pair * 64 + (4 * a + b) % 8, 8, stride=8), :]
-                    for b in range(4)
-                ]
+                mat, adm = [], []
+                for b in range(4):
+                    entry = 4 * a + b
+                    at = (entry // 8) * (elems // 16) + pair * 64 + entry % 8
+                    mat.append(mass[pl.ds(at, 8, stride=8), :])
+                    adm.append(adv[pl.ds(at, 8, stride=8), :])
                 for c in range(6):
                     g = adm[0] * tdir[0][c] + mat[0] * gin[0][c]
                     d = adm[0] * wsum[0][c] + mat[0] * usum[0][c]
@@ -359,17 +378,19 @@
             score = 0.25 * score
             for a in range(4):
                 terms[a, pl.ds(6, 8, stride=TERM), :] = score
-
             live = (pair * 8 + sub) * LANES + lane < count
             for k in range(4):
-                index_rows[0, pl.ds(8 * k, 8), :] = places[k].astype(jnp.float32)
-                index_rows[1, pl.ds(8 * k, 8), :] = jnp.where(live, rels[k] >> 7, -1).astype(
+                rel = relative(pair, k)
+                index_rows[0, pl.ds(8 * k, 8), :] = (rel & (LANES - 1)).astype(jnp.float32)
+                index_rows[1, pl.ds(8 * k, 8), :] = jnp.where(live, rel >> 7, -1).astype(
                     jnp.float32
                 )
+
+        def scatter(pair, terms, index_rows):
+            listed = (2 * pair) % LISTS
             for which, start in enumerate(starts_of(pair)):
-                total = jnp.zeros((4 * 2 * TERM, LANES), jnp.float32)
+                lefts, rights = [], []
                 for k in range(4):
-                    lefts, rights = [], []
                     for j in range(groups):
                         g = which * groups + j
                         part = two_parts(terms[k, pl.ds(g * TERM, TERM), :])
@@ -385,12 +406,12 @@
                             )
                         )
                         rights.append(factor(jnp.concatenate([place] * 8, axis=0)))
-                    total = total + lax.dot_general(
-                        jnp.concatenate(lefts, axis=1),
-                        jnp.concatenate(rights, axis=1),
-                        contract,
-                        preferred_element_type=jnp.float32,
-                    )
+                total = lax.dot_general(
+                    jnp.concatenate(lefts, axis=1),
+                    jnp.concatenate(rights, axis=1),
+                    contract,
+                    preferred_element_type=jnp.float32,
+                )
                 sums = [
                     total[16 * i : 16 * i + 8] + total[16 * i + 8 : 16 * i + 16]
                     for i in range(4)
@@ -411,27 +432,38 @@
                 gout[listed + which] = gout[listed + which] + sums[WIN]
 
         turns = LISTS // 2
-        rounds = steps // turns
+
+        @pl.loop(0, LISTS)
+        def _(k):
+            @pl.when(inside(me - list_offset(k)))
+            def _():
+                push(k).wait_recv()
+
+        def give_back(turn):
+            for which in range(2):
+                k = 2 * turn + which
+
+                @pl.when(inside(me - list_offset(k)) & (k >= 0))
+                def _():
+                    push_back(k).start()
+
+        gather_ghosts(0, gtable0, merged0)
+        gather_ghosts(turns, gtable1, merged1)
 
         @pl.loop(0, turns)
         def _(turn):
-            for which in range(2):
-                k = 2 * turn + which
-
-                @pl.when(inside(me - list_offset(k)))
-                def _():
-                    push(k).wait_recv()
-
-            @pl.loop(0, rounds)
-            def _(r):
-                visit(turn + r * turns)
-
-            for which in range(2):
-                k = 2 * turn + which
-
-                @pl.when(inside(me - list_offset(k)))
-                def _():
-                    push_back(k).start()
+            later = jnp.minimum(turn + 1, turns - 1)
+            before = jnp.maximum(turn - 1, 0)
+            algebra(turn, merged0, terms0, index0)
+            scatter(before + turns, terms1, index1)
+            gather_ghosts(later, gtable0, merged0)
+            algebra(turn + turns, merged1, terms1, index1)
+            scatter(turn, terms0, index0)
+            gather_ghosts(later + turns, gtable1, merged1)
+            give_back(turn - 1)
+
+        scatter(2 * turns - 1, terms1, index1)
+        give_back(turns - 1)
 
         @pl.loop(0, LISTS)
         def _(k):
@@ -559,10 +591,19 @@
             pltpu.VMEM((LISTS, ROWS, LANES), f32),
             pltpu.VMEM((LISTS, ROWS, LANES), f32),
             pltpu.VMEM((2, WIN * ROWS, LANES), f32),
+            pltpu.VMEM((2, WIN * ROWS, LANES), f32),
+            pltpu.VMEM((20 * WIN, 8, LANES), f32),
+            pltpu.VMEM((20 * WIN, 8, LANES), f32),
             pltpu.VMEM((steps, 80, 8, LANES), f32),
             pltpu.VMEM((elems // 16, LANES), f32),
             pltpu.VMEM((elems // LANES, LANES), f32),
+            pltpu.VMEM((20, 8, LANES), f32),
+            pltpu.VMEM((20, 8, LANES), f32),
+            pltpu.VMEM((80, 8, LANES), f32),
+            pltpu.VMEM((80, 8, LANES), f32),
             pltpu.VMEM((2, 32, LANES), f32),
+            pltpu.VMEM((2, 32, LANES), f32),
+            pltpu.VMEM((4, 8 * TERM, LANES), f32),
             pltpu.VMEM((4, 8 * TERM, LANES), f32),
             pltpu.VMEM(((chunks + 1) * TERM, LANES), f32),
             pltpu.VMEM((LISTS, TERM, LANES), f32),
@@ -577,7 +618,7 @@
         compiler_params=pltpu.CompilerParams(
             collective_id=0,
             has_side_effects=True,
-            vmem_limit_bytes=48 * 1024 * 1024,
+            vmem_limit_bytes=62 * 1024 * 1024,
         ),
     )(*args)
     return res, hess.reshape(nodes)

time: 50.7 us -> 35.9 us (0.71)
  the two profiles are of different devices: /device:TPU:6 before, /device:TPU:7 now
where the time goes in v2:
time: 35.9 us; the launch traced here: 35.8 us
  Pallas kernels  32.3 us (90%)
  local copies, waits for them, and re-layouts  2.15 us (6%)
  between operations  1.3 us (4%)
    pallas_call x1, Pallas kernels, shards(): pl.pallas_call(make_kernel(ndev, nodes, elems), out_shape=(jax.ShapeDtype...  32.3 us
    unnamed x4, local copies, waits for them, and re-layouts  2.15 us

profile of v2, /device:TPU:7, one launch (start us, length us, event | category | flops | bytes accessed | tf_op | source)
XLA Modules:
  0.0 35.8 jit_solution(13276438569191161938)
XLA Ops:
  1.3 32.3 %shard_map.122 = (f32[6,3072]{1,0:T(8,128)}, f32[24,128]{1,0:T(8,128)}) custom-call(f32[6,3072]{1,0:T(8,128)} %stress_hbm.1, f32[6,3072]{1,0:T(8,128)} %dir_hbm.1, f32[6,3072]{1,0:T(8,128)} %adj_hbm.1, f32[24,128]{1,0:T(8,128)} %bitcast.23, f32[24,128]{1,0:T(8,128)} %bitcast.24, s32[512,128]{1,0:T(8,128)} %bitcast.21, f32[2048,128]{1,0:T(8,128)} %bitcast.19, ...), custom_call_target="tpu_custom_call" | custom-call | tf_op jit(solution)/shard_map/pallas_call | solution.py:569
  33.6 0.0 copy-start
  33.6 1.5 %copy.17 = f32[6,3072]{1,0:T(8,128)} copy(f32[6,3072]{1,0:T(8,128)} %get-tuple-element.8) | data formatting | bytes 147456
  35.2 0.0 copy-done
  35.2 0.6 %copy.18 = f32[3072]{0:T(1024)} copy(f32[3072]{0:T(1024)S(1)} %bitcast.22) | data formatting | bytes 24576
Async XLA Ops:
  33.6 1.6 %copy-start = (f32[24,128]{1,0:T(8,128)S(1)}, f32[24,128]{1,0:T(8,128)}, u32[]{:S(2)}) copy-start(f32[24,128]{1,0:T(8,128)} %get-tuple-element.5) | copy-start | bytes 36868

commit v3 on v2

--- a/solution.py
+++ b/solution.py
@@ -47,9 +47,8 @@
 
 
 def two_parts(values):
-    high = values.astype(jnp.bfloat16)
-    low = (values - high.astype(jnp.float32)).astype(jnp.bfloat16)
-    return jnp.concatenate([high, low], axis=0)
+    high = values.astype(jnp.bfloat16).astype(jnp.float32)
+    return jnp.concatenate([high, values - high], axis=0).astype(jnp.bfloat16)
 
 
 def symmetric_product(left, right):
@@ -69,9 +68,9 @@
     chunks = nodes // LANES
     nblocks = elems // ELEM_BLOCK
     groups = ELEM_BLOCK // LANES
-    steps = nblocks // 2
     span = max(nblocks - 1, 1)
     window = WIN * LANES
+    turns = LISTS // 2
 
     def kernel(
         stress_hbm,
@@ -106,17 +105,26 @@
         rolled1,
         table0,
         table1,
-        values,
-        gradv,
-        grad8,
+        owned0,
+        owned1,
+        vel0,
+        vel1,
+        vel80,
+        vel81,
+        mvel0,
+        mvel1,
+        mvel80,
+        mvel81,
         gtable0,
         gtable1,
         merged0,
         merged1,
-        index0,
-        index1,
+        index,
+        rels,
         terms0,
         terms1,
+        parts0,
+        parts1,
         acc,
         gout,
         returned,
@@ -175,13 +183,48 @@
             cut = pl.ds(c * LANES, LANES)
             for base in (TAU, DIR, ADJ):
                 fields[pl.ds(c * ROWS + base, 8), :] = zeros
-            fields[pl.ds(c * ROWS + TAU, 6), :] = stress[:, cut]
+            fields[pl.ds(c * ROWS + TAU, 6), :] = 0.5 * KAPPA * stress[:, cut]
             fields[pl.ds(c * ROWS + LAM, 1), :] = relax[pl.ds(c, 1), :]
             fields[pl.ds(c * ROWS + DLAM, 1), :] = rdir[pl.ds(c, 1), :]
             fields[pl.ds(c * ROWS + DIR, 6), :] = sdir[:, cut]
             fields[pl.ds(c * ROWS + ADJ, 6), :] = adjoint[:, cut]
         for base in (TAU, DIR, ADJ):
             fields[pl.ds(chunks * ROWS + base, 8), :] = zeros
+
+        def starts_of(pair):
+            one = (2 * pair) * (nodes - window) // span
+            two = (2 * pair + 1) * (nodes - window) // span
+            return one, two
+
+        def relative(pair, k):
+            one, two = starts_of(pair)
+            lists_one = (2 * pair) % LISTS
+            node = conn[pl.ds(pair * 32 + k, 8, stride=4), :]
+            start = jnp.where(upper, two, one)
+            ghost0 = nodes + LANES * jnp.where(upper, lists_one + 1, lists_one) - window
+            return node - jnp.where(node >= nodes, ghost0, start)
+
+        count = count_ref[0]
+        columns = lax.broadcasted_iota(jnp.int32, (LANES, LANES), 0).astype(jnp.bfloat16)
+        one16 = jnp.ones((LANES, LANES), jnp.bfloat16)
+        zero16 = jnp.zeros((LANES, LANES), jnp.bfloat16)
+        contract = (((1,), (1,)), ((), ()))
+
+        def factor(place_row):
+            return jnp.where(columns == place_row, one16, zero16)
+
+        def mark(pair):
+            live = (pair * 8 + sub) * LANES + lane < count
+            for k in range(4):
+                rel = relative(pair, k)
+                rels[pair, k] = rel
+                index[pair, 0, pl.ds(8 * k, 8), :] = (rel & (LANES - 1)).astype(jnp.float32)
+                index[pair, 1, pl.ds(8 * k, 8), :] = jnp.where(live, rel >> 7, -1).astype(
+                    jnp.float32
+                )
+
+        for load in loads[6:7]:
+            load.wait()
 
         @pl.loop(0, LISTS)
         def _(k):
@@ -196,6 +239,7 @@
                     picked[t] = jnp.where(here, got, picked[t])
             for t in range(3):
                 payload[k, pl.ds(8 * t, 8), :] = picked[t]
+            mark(k)
 
         first_up = jnp.minimum(HOPS, ndev - 1 - me)
         first_down = jnp.minimum(HOPS, me)
@@ -233,29 +277,31 @@
             acc[pl.ds(i * TERM, TERM), :] = zeros
         for i in range(LISTS):
             gout[i] = zeros
+        for i in range(2 * WIN):
+            parts0[i] = zeros
         for terms in (terms0, terms1):
             for k in range(4):
                 for g in range(8):
                     terms[k, pl.ds(g * TERM, TERM), :] = zeros
-        for k in range(4):
-            index1[0, pl.ds(8 * k, 8), :] = zeros
-            index1[1, pl.ds(8 * k, 8), :] = zeros - 1.0
-
-        for load in loads[6:8]:
-            load.wait()
-
-        def starts_of(pair):
-            one = (2 * pair) * (nodes - window) // span
-            two = (2 * pair + 1) * (nodes - window) // span
-            return one, two
-
-        def relative(pair, k):
-            one, two = starts_of(pair)
-            lists_one = (2 * pair) % LISTS
-            node = conn[pl.ds(pair * 32 + k, 8, stride=4), :]
-            start = jnp.where(upper, two, one)
-            ghost0 = nodes + LANES * jnp.where(upper, lists_one + 1, lists_one) - window
-            return node - jnp.where(node >= nodes, ghost0, start)
+        loads[7].wait()
+
+        def weave(one, two):
+            spent = [0, 0]
+            parts = [one, two]
+            while parts[0] is not None or parts[1] is not None:
+                which = 0 if spent[0] <= spent[1] else 1
+                if parts[which] is None:
+                    which = 1 - which
+                cost = next(parts[which], None)
+                if cost is None:
+                    parts[which] = None
+                else:
+                    spent[which] += cost
+
+        def run(*parts):
+            for part in parts:
+                for _ in part:
+                    pass
 
         def prepare(pair, rolled, table):
             for which, start in enumerate(starts_of(pair)):
@@ -277,6 +323,7 @@
                         rolled[which, pl.ds(i * ROWS + 8 * t, 8), :] = jnp.where(
                             keep, turned[i], turned[i + 1]
                         )
+            yield 50
             for n, row in enumerate(FIELD_ROWS):
                 for i in range(WIN):
                     table[n * WIN + i] = jnp.where(
@@ -284,81 +331,75 @@
                         row_of(rolled.at[1], i * ROWS + row),
                         row_of(rolled.at[0], i * ROWS + row),
                     )
-
-        def gather_owned(pair, table):
+            yield 20
+
+        def gather_owned(pair, table, owned, vel, vel8):
             for k in range(4):
-                rel = relative(pair, k)
+                rel = rels[pair, k]
                 place = rel & (LANES - 1)
                 first = rel < LANES
                 second = rel < 2 * LANES
                 for n in range(20):
                     a, b, c = [pick_lanes(table[n * WIN + i], place) for i in range(WIN)]
-                    values[pair, k * 20 + n] = jnp.where(first, a, jnp.where(second, b, c))
+                    owned[k * 20 + n] = jnp.where(first, a, jnp.where(second, b, c))
+                    if n % 4 == 3:
+                        yield 24
             for j in range(8):
                 cut = pl.ds(pl.multiple_of((pair * 8 + j) * LANES, LANES), LANES)
-                gradv[pl.ds(pl.multiple_of((pair * 8 + j) * 8, 8), 8), :] = grad[0:8, cut]
-                grad8[pl.ds(pair * 8 + j, 1), :] = grad[8:9, cut]
-
-        prepare(0, rolled0, table0)
-
-        @pl.loop(0, steps // 2)
-        def _(i):
-            gather_owned(2 * i, table0)
-            prepare(2 * i + 1, rolled1, table1)
-            gather_owned(2 * i + 1, table1)
-            prepare(jnp.minimum(2 * i + 2, steps - 1), rolled0, table0)
+                vel[pl.ds(j * 8, 8), :] = grad[0:8, cut]
+                vel8[pl.ds(j, 1), :] = grad[8:9, cut]
+            yield 8
+
+        run(prepare(0, rolled0, table0), prepare(turns, rolled1, table1))
+        run(gather_owned(0, table0, owned0, vel0, vel80), prepare(1, rolled0, table0))
+        run(gather_owned(turns, table1, owned1, vel1, vel81), prepare(turns + 1, rolled1, table1))
 
         for load in loads[8:]:
             load.wait()
 
-        count = count_ref[0]
-        columns = lax.broadcasted_iota(jnp.int32, (LANES, LANES), 0).astype(jnp.bfloat16)
-        one16 = jnp.ones((LANES, LANES), jnp.bfloat16)
-        zero16 = jnp.zeros((LANES, LANES), jnp.bfloat16)
-        contract = (((1,), (1,)), ((), ()))
-
-        def factor(place_row):
-            return jnp.where(columns == place_row, one16, zero16)
-
-        def gather_ghosts(pair, gtable, merged):
+        def gather_ghosts(pair, gtable, owned, vel_in, vel8_in, merged, vel, vel8):
             listed = (2 * pair) % LISTS
             for n, row in enumerate(FIELD_ROWS):
                 gtable[n] = jnp.where(
                     upper, row_of(ghosts.at[listed + 1], row), row_of(ghosts.at[listed], row)
                 )
+            vel[...] = vel_in[...]
+            vel8[...] = vel8_in[...]
+            yield 15
             for k in range(4):
-                rel = relative(pair, k)
+                rel = rels[pair, k]
                 place = rel & (LANES - 1)
                 ghostly = rel >= window
                 for n in range(20):
                     merged[k * 20 + n] = jnp.where(
-                        ghostly, pick_lanes(gtable[n], place), values[pair, k * 20 + n]
+                        ghostly, pick_lanes(gtable[n], place), owned[k * 20 + n]
                     )
-
-        def algebra(pair, merged, terms, index_rows):
-            got = [[merged[k * 20 + n] for n in range(20)] for k in range(4)]
-            lam_e = 0.25 * (got[0][6] + got[1][6] + got[2][6] + got[3][6])
-            dlam_e = 0.25 * (got[0][7] + got[1][7] + got[2][7] + got[3][7])
-            vel = [
-                gradv[pl.ds(pair * 64 + i, 8, stride=8), :] for i in range(8)
-            ] + [grad8[pl.ds(pl.multiple_of(pair * 8, 8), 8), :]]
+                    if n % 10 == 9:
+                        yield 20
+
+        def algebra(pair, merged, vel_rows, vel8, terms):
+            def got(k, n):
+                return merged[k * 20 + n]
+
+            lam_e = 0.25 * (got(0, 6) + got(1, 6) + got(2, 6) + got(3, 6))
+            dlam4 = got(0, 7) + got(1, 7) + got(2, 7) + got(3, 7)
+            vel = [vel_rows[pl.ds(i, 8, stride=8), :] for i in range(8)] + [vel8[...]]
             tdir, gin, wsum, usum = [], [], [], []
             for k in range(4):
-                tau = got[k][0:6]
-                t = got[k][8:14]
-                half = [KAPPA * s for s in tau]
-                quarter = [0.5 * s for s in half]
+                tau = [got(k, c) for c in range(6)]
+                t = [got(k, 8 + c) for c in range(6)]
+                left_b = [
+                    [tau[LAYOUT[r][c]] - vel[3 * r + c] for c in range(3)] for r in range(3)
+                ]
                 left_g = [
-                    [half[LAYOUT[r][c]] - vel[3 * r + c] for c in range(3)] for r in range(3)
-                ]
-                left_b = [
-                    [quarter[LAYOUT[r][c]] - vel[3 * r + c] for c in range(3)] for r in range(3)
+                    [left_b[r][c] + tau[LAYOUT[r][c]] for c in range(3)] for r in range(3)
                 ]
                 b_in = symmetric_product(left_b, tau)
                 tdir.append(t)
                 gin.append(symmetric_product(left_g, t))
-                wsum.append([dlam_e * s for s in tau])
-                usum.append([t[c] + dlam_e * b_in[c] for c in range(6)])
+                wsum.append([dlam4 * s for s in tau])
+                usum.append([t[c] + dlam4 * b_in[c] for c in range(6)])
+                yield 38
             score = zeros
             for a in range(4):
                 mat, adm = [], []
@@ -373,29 +414,26 @@
                     for b in range(1, 4):
                         g = g + (adm[b] * tdir[b][c] + mat[b] * gin[b][c])
                         d = d + (adm[b] * wsum[b][c] + mat[b] * usum[b][c])
-                    score = score + got[a][14 + c] * g
+                    score = score + got(a, 14 + c) * g
                     terms[a, pl.ds(c, 8, stride=TERM), :] = d + lam_e * g
+                    if c % 2 == 1:
+                        yield 17
             score = 0.25 * score
             for a in range(4):
                 terms[a, pl.ds(6, 8, stride=TERM), :] = score
-            live = (pair * 8 + sub) * LANES + lane < count
-            for k in range(4):
-                rel = relative(pair, k)
-                index_rows[0, pl.ds(8 * k, 8), :] = (rel & (LANES - 1)).astype(jnp.float32)
-                index_rows[1, pl.ds(8 * k, 8), :] = jnp.where(live, rel >> 7, -1).astype(
-                    jnp.float32
-                )
-
-        def scatter(pair, terms, index_rows):
+            yield 2
+
+        def scatter(pair, terms, parts):
             listed = (2 * pair) % LISTS
-            for which, start in enumerate(starts_of(pair)):
+            for which in range(2):
                 lefts, rights = [], []
                 for k in range(4):
                     for j in range(groups):
                         g = which * groups + j
                         part = two_parts(terms[k, pl.ds(g * TERM, TERM), :])
-                        chunk = row_of(index_rows.at[1], 8 * k + g, 16).astype(jnp.bfloat16)
-                        place = row_of(index_rows.at[0], 8 * k + g, 16).astype(jnp.bfloat16)
+                        chunk = row_of(index.at[pair, 1], 8 * k + g, 16).astype(jnp.bfloat16)
+                        place = row_of(index.at[pair, 0], 8 * k + g, 16).astype(jnp.bfloat16)
+                        rights.append(factor(jnp.concatenate([place] * 8, axis=0)))
                         lefts.append(
                             jnp.concatenate(
                                 [
@@ -405,7 +443,7 @@
                                 axis=0,
                             )
                         )
-                        rights.append(factor(jnp.concatenate([place] * 8, axis=0)))
+                    yield 32
                 total = lax.dot_general(
                     jnp.concatenate(lefts, axis=1),
                     jnp.concatenate(rights, axis=1),
@@ -416,9 +454,16 @@
                     total[16 * i : 16 * i + 8] + total[16 * i + 8 : 16 * i + 16]
                     for i in range(4)
                 ]
+                for i in range(WIN):
+                    parts[which * WIN + i] = sums[i]
+                gout[listed + which] = gout[listed + which] + sums[WIN]
+                yield 4
+
+        def fold(pair, parts):
+            for which, start in enumerate(starts_of(pair)):
                 chunk0 = start // LANES
                 shift = start % LANES
-                turned = [pltpu.roll(sums[i], shift, 1) for i in range(WIN)]
+                turned = [pltpu.roll(parts[which * WIN + i], shift, 1) for i in range(WIN)]
                 later = lane >= shift
                 for i in range(WIN + 1):
                     if i == 0:
@@ -429,9 +474,11 @@
                         add = jnp.where(later, turned[i], turned[i - 1])
                     at = pl.ds(pl.multiple_of((chunk0 + i) * TERM, TERM), TERM)
                     acc[at, :] = acc[at, :] + add
-                gout[listed + which] = gout[listed + which] + sums[WIN]
-
-        turns = LISTS // 2
+                yield 8
+
+        def both(one, two):
+            yield from one
+            yield from two
 
         @pl.loop(0, LISTS)
         def _(k):
@@ -447,22 +494,54 @@
                 def _():
                     push_back(k).start()
 
-        gather_ghosts(0, gtable0, merged0)
-        gather_ghosts(turns, gtable1, merged1)
+        def merge(turn, half):
+            if half == 0:
+                return gather_ghosts(
+                    turn, gtable0, owned0, vel0, vel80, merged0, mvel0, mvel80
+                )
+            return gather_ghosts(
+                turn + turns, gtable1, owned1, vel1, vel81, merged1, mvel1, mvel81
+            )
+
+        def look_ahead(turn, half):
+            after = jnp.minimum(turn + 1, turns - 1)
+            if half == 0:
+                yield from gather_owned(turn, table0, owned0, vel0, vel80)
+                yield from prepare(after, rolled0, table0)
+            else:
+                yield from gather_owned(turn + turns, table1, owned1, vel1, vel81)
+                yield from prepare(after + turns, rolled1, table1)
+
+        run(merge(0, 0), look_ahead(1, 0))
 
         @pl.loop(0, turns)
         def _(turn):
-            later = jnp.minimum(turn + 1, turns - 1)
             before = jnp.maximum(turn - 1, 0)
-            algebra(turn, merged0, terms0, index0)
-            scatter(before + turns, terms1, index1)
-            gather_ghosts(later, gtable0, merged0)
-            algebra(turn + turns, merged1, terms1, index1)
-            scatter(turn, terms0, index0)
-            gather_ghosts(later + turns, gtable1, merged1)
+            one = jnp.minimum(turn + 1, turns - 1)
+            two = jnp.minimum(turn + 2, turns - 1)
+            run(fold(before, parts0))
+            weave(
+                both(merge(turn, 1), look_ahead(one, 1)),
+                both(
+                    algebra(turn, merged0, mvel0, mvel80, terms0),
+                    scatter(before + turns, terms1, parts1),
+                ),
+            )
+            run(fold(before + turns, parts1))
+            weave(
+                both(merge(one, 0), look_ahead(two, 0)),
+                both(
+                    algebra(turn + turns, merged1, mvel1, mvel81, terms1),
+                    scatter(turn, terms0, parts0),
+                ),
+            )
             give_back(turn - 1)
 
-        scatter(2 * turns - 1, terms1, index1)
+        run(
+            scatter(2 * turns - 1, terms1, parts1),
+            fold(turns - 1, parts0),
+            fold(2 * turns - 1, parts1),
+        )
         give_back(turns - 1)
 
         @pl.loop(0, LISTS)
@@ -545,7 +624,6 @@
     nodes = stress.shape[1]
     elems = connect.shape[1]
     chunks = nodes // LANES
-    steps = elems // ELEM_BLOCK // 2
     f32, i32 = jnp.float32, jnp.int32
 
     def by_groups(matrix, rows):
@@ -594,17 +672,26 @@
             pltpu.VMEM((2, WIN * ROWS, LANES), f32),
             pltpu.VMEM((20 * WIN, 8, LANES), f32),
             pltpu.VMEM((20 * WIN, 8, LANES), f32),
-            pltpu.VMEM((steps, 80, 8, LANES), f32),
-            pltpu.VMEM((elems // 16, LANES), f32),
-            pltpu.VMEM((elems // LANES, LANES), f32),
+            pltpu.VMEM((80, 8, LANES), f32),
+            pltpu.VMEM((80, 8, LANES), f32),
+            pltpu.VMEM((64, LANES), f32),
+            pltpu.VMEM((64, LANES), f32),
+            pltpu.VMEM((8, LANES), f32),
+            pltpu.VMEM((8, LANES), f32),
+            pltpu.VMEM((64, LANES), f32),
+            pltpu.VMEM((64, LANES), f32),
+            pltpu.VMEM((8, LANES), f32),
+            pltpu.VMEM((8, LANES), f32),
             pltpu.VMEM((20, 8, LANES), f32),
             pltpu.VMEM((20, 8, LANES), f32),
             pltpu.VMEM((80, 8, LANES), f32),
             pltpu.VMEM((80, 8, LANES), f32),
-            pltpu.VMEM((2, 32, LANES), f32),
-            pltpu.VMEM((2, 32, LANES), f32),
+            pltpu.VMEM((LISTS, 2, 32, LANES), f32),
+            pltpu.VMEM((LISTS, 4, 8, LANES), i32),
             pltpu.VMEM((4, 8 * TERM, LANES), f32),
             pltpu.VMEM((4, 8 * TERM, LANES), f32),
+            pltpu.VMEM((2 * WIN, TERM, LANES), f32),
+            pltpu.VMEM((2 * WIN, TERM, LANES), f32),
             pltpu.VMEM(((chunks + 1) * TERM, LANES), f32),
             pltpu.VMEM((LISTS, TERM, LANES), f32),
             pltpu.VMEM((LISTS, TERM, LANES), f32),

time: 35.9 us -> 36.5 us (1.017)
  Pallas kernels: 32.3 us -> 32.9 us
    pallas_call x1, Pallas kernels: 32.3 us -> 32.9 us  [shards(): pl.pallas_call(make_kernel(ndev, nodes, elems), out_shape=(jax.ShapeDtype...]
where the time goes in v3:
time: 36.5 us; the launch traced here: 36.4 us
  Pallas kernels  32.9 us (90%)
  local copies, waits for them, and re-layouts  2.15 us (6%)
  between operations  1.3 us (4%)
    pallas_call x1, Pallas kernels, shards(): pl.pallas_call(make_kernel(ndev, nodes, elems), out_shape=(jax.ShapeDtype...  32.9 us
    unnamed x4, local copies, waits for them, and re-layouts  2.15 us

profile of v3, /device:TPU:7, one launch (start us, length us, event | category | flops | bytes accessed | tf_op | source)
XLA Modules:
  0.0 36.4 jit_solution(8795689622719227806)
XLA Ops:
  1.3 32.9 %shard_map.122 = (f32[6,3072]{1,0:T(8,128)}, f32[24,128]{1,0:T(8,128)}) custom-call(f32[6,3072]{1,0:T(8,128)} %stress_hbm.1, f32[6,3072]{1,0:T(8,128)} %dir_hbm.1, f32[6,3072]{1,0:T(8,128)} %adj_hbm.1, f32[24,128]{1,0:T(8,128)} %bitcast.23, f32[24,128]{1,0:T(8,128)} %bitcast.24, s32[512,128]{1,0:T(8,128)} %bitcast.21, f32[2048,128]{1,0:T(8,128)} %bitcast.19, ...), custom_call_target="tpu_custom_call" | custom-call | tf_op jit(solution)/shard_map/pallas_call | solution.py:647
  34.2 0.0 copy-start
  34.2 1.5 %copy.17 = f32[6,3072]{1,0:T(8,128)} copy(f32[6,3072]{1,0:T(8,128)} %get-tuple-element.8) | data formatting | bytes 147456
  35.7 0.0 copy-done
  35.8 0.6 %copy.18 = f32[3072]{0:T(1024)} copy(f32[3072]{0:T(1024)S(1)} %bitcast.22) | data formatting | bytes 24576
Async XLA Ops:
  34.2 1.6 %copy-start = (f32[24,128]{1,0:T(8,128)S(1)}, f32[24,128]{1,0:T(8,128)}, u32[]{:S(2)}) copy-start(f32[24,128]{1,0:T(8,128)} %get-tuple-element.5) | copy-start | bytes 36868

commit v4 on v3

--- a/solution.py
+++ b/solution.py
@@ -105,16 +105,9 @@
         rolled1,
         table0,
         table1,
-        owned0,
-        owned1,
-        vel0,
-        vel1,
-        vel80,
-        vel81,
-        mvel0,
-        mvel1,
-        mvel80,
-        mvel81,
+        values,
+        vel,
+        vel8,
         gtable0,
         gtable1,
         merged0,
@@ -123,8 +116,6 @@
         rels,
         terms0,
         terms1,
-        parts0,
-        parts1,
         acc,
         gout,
         returned,
@@ -277,8 +268,6 @@
             acc[pl.ds(i * TERM, TERM), :] = zeros
         for i in range(LISTS):
             gout[i] = zeros
-        for i in range(2 * WIN):
-            parts0[i] = zeros
         for terms in (terms0, terms1):
             for k in range(4):
                 for g in range(8):
@@ -333,7 +322,7 @@
                     )
             yield 20
 
-        def gather_owned(pair, table, owned, vel, vel8):
+        def gather_owned(pair, table):
             for k in range(4):
                 rel = rels[pair, k]
                 place = rel & (LANES - 1)
@@ -341,30 +330,34 @@
                 second = rel < 2 * LANES
                 for n in range(20):
                     a, b, c = [pick_lanes(table[n * WIN + i], place) for i in range(WIN)]
-                    owned[k * 20 + n] = jnp.where(first, a, jnp.where(second, b, c))
+                    values[pair, k * 20 + n] = jnp.where(first, a, jnp.where(second, b, c))
                     if n % 4 == 3:
                         yield 24
             for j in range(8):
                 cut = pl.ds(pl.multiple_of((pair * 8 + j) * LANES, LANES), LANES)
-                vel[pl.ds(j * 8, 8), :] = grad[0:8, cut]
-                vel8[pl.ds(j, 1), :] = grad[8:9, cut]
+                vel[pair, pl.ds(j * 8, 8), :] = grad[0:8, cut]
+                vel8[pair, pl.ds(j, 1), :] = grad[8:9, cut]
             yield 8
 
-        run(prepare(0, rolled0, table0), prepare(turns, rolled1, table1))
-        run(gather_owned(0, table0, owned0, vel0, vel80), prepare(1, rolled0, table0))
-        run(gather_owned(turns, table1, owned1, vel1, vel81), prepare(turns + 1, rolled1, table1))
+        run(prepare(0, rolled0, table0))
+
+        @pl.loop(0, turns)
+        def _(i):
+            weave(gather_owned(2 * i, table0), prepare(2 * i + 1, rolled1, table1))
+            weave(
+                gather_owned(2 * i + 1, table1),
+                prepare(jnp.minimum(2 * i + 2, 2 * turns - 1), rolled0, table0),
+            )
 
         for load in loads[8:]:
             load.wait()
 
-        def gather_ghosts(pair, gtable, owned, vel_in, vel8_in, merged, vel, vel8):
+        def gather_ghosts(pair, gtable, merged):
             listed = (2 * pair) % LISTS
             for n, row in enumerate(FIELD_ROWS):
                 gtable[n] = jnp.where(
                     upper, row_of(ghosts.at[listed + 1], row), row_of(ghosts.at[listed], row)
                 )
-            vel[...] = vel_in[...]
-            vel8[...] = vel8_in[...]
             yield 15
             for k in range(4):
                 rel = rels[pair, k]
@@ -372,24 +365,24 @@
                 ghostly = rel >= window
                 for n in range(20):
                     merged[k * 20 + n] = jnp.where(
-                        ghostly, pick_lanes(gtable[n], place), owned[k * 20 + n]
+                        ghostly, pick_lanes(gtable[n], place), values[pair, k * 20 + n]
                     )
                     if n % 10 == 9:
                         yield 20
 
-        def algebra(pair, merged, vel_rows, vel8, terms):
+        def algebra(pair, merged, terms):
             def got(k, n):
                 return merged[k * 20 + n]
 
             lam_e = 0.25 * (got(0, 6) + got(1, 6) + got(2, 6) + got(3, 6))
             dlam4 = got(0, 7) + got(1, 7) + got(2, 7) + got(3, 7)
-            vel = [vel_rows[pl.ds(i, 8, stride=8), :] for i in range(8)] + [vel8[...]]
+            grads = [vel[pair, pl.ds(i, 8, stride=8), :] for i in range(8)] + [vel8[pair]]
             tdir, gin, wsum, usum = [], [], [], []
             for k in range(4):
                 tau = [got(k, c) for c in range(6)]
                 t = [got(k, 8 + c) for c in range(6)]
                 left_b = [
-                    [tau[LAYOUT[r][c]] - vel[3 * r + c] for c in range(3)] for r in range(3)
+                    [tau[LAYOUT[r][c]] - grads[3 * r + c] for c in range(3)] for r in range(3)
                 ]
                 left_g = [
                     [left_b[r][c] + tau[LAYOUT[r][c]] for c in range(3)] for r in range(3)
@@ -423,9 +416,9 @@
                 terms[a, pl.ds(6, 8, stride=TERM), :] = score
             yield 2
 
-        def scatter(pair, terms, parts):
+        def scatter(pair, terms):
             listed = (2 * pair) % LISTS
-            for which in range(2):
+            for which, start in enumerate(starts_of(pair)):
                 lefts, rights = [], []
                 for k in range(4):
                     for j in range(groups):
@@ -454,16 +447,9 @@
                     total[16 * i : 16 * i + 8] + total[16 * i + 8 : 16 * i + 16]
                     for i in range(4)
                 ]
-                for i in range(WIN):
-                    parts[which * WIN + i] = sums[i]
-                gout[listed + which] = gout[listed + which] + sums[WIN]
-                yield 4
-
-        def fold(pair, parts):
-            for which, start in enumerate(starts_of(pair)):
                 chunk0 = start // LANES
                 shift = start % LANES
-                turned = [pltpu.roll(parts[which * WIN + i], shift, 1) for i in range(WIN)]
+                turned = [pltpu.roll(sums[i], shift, 1) for i in range(WIN)]
                 later = lane >= shift
                 for i in range(WIN + 1):
                     if i == 0:
@@ -474,86 +460,78 @@
                         add = jnp.where(later, turned[i], turned[i - 1])
                     at = pl.ds(pl.multiple_of((chunk0 + i) * TERM, TERM), TERM)
                     acc[at, :] = acc[at, :] + add
-                yield 8
+                gout[listed + which] = gout[listed + which] + sums[WIN]
+                yield 10
 
         def both(one, two):
             yield from one
             yield from two
 
-        @pl.loop(0, LISTS)
-        def _(k):
-            @pl.when(inside(me - list_offset(k)))
-            def _():
-                push(k).wait_recv()
+        def at_turn(step):
+            return (step + turns // 2) % turns
+
+        def await_ghosts(turn):
+            for which in range(2):
+                k = 2 * turn + which
+
+                @pl.when(inside(me - list_offset(k)))
+                def _():
+                    push(k).wait_recv()
 
         def give_back(turn):
             for which in range(2):
                 k = 2 * turn + which
 
-                @pl.when(inside(me - list_offset(k)) & (k >= 0))
+                @pl.when(inside(me - list_offset(k)))
                 def _():
                     push_back(k).start()
 
-        def merge(turn, half):
-            if half == 0:
-                return gather_ghosts(
-                    turn, gtable0, owned0, vel0, vel80, merged0, mvel0, mvel80
-                )
-            return gather_ghosts(
-                turn + turns, gtable1, owned1, vel1, vel81, merged1, mvel1, mvel81
+        first = at_turn(0)
+        await_ghosts(first)
+        run(gather_ghosts(first, gtable0, merged0))
+
+        @pl.loop(0, turns)
+        def _(step):
+            turn = at_turn(step)
+            after = at_turn(jnp.minimum(step + 1, turns - 1))
+            before = at_turn(jnp.maximum(step - 1, 0))
+
+            @pl.when(step < turns - 1)
+            def _():
+                await_ghosts(after)
+
+            weave(
+                gather_ghosts(turn + turns, gtable1, merged1),
+                both(algebra(turn, merged0, terms0), scatter(before + turns, terms1)),
             )
-
-        def look_ahead(turn, half):
-            after = jnp.minimum(turn + 1, turns - 1)
-            if half == 0:
-                yield from gather_owned(turn, table0, owned0, vel0, vel80)
-                yield from prepare(after, rolled0, table0)
-            else:
-                yield from gather_owned(turn + turns, table1, owned1, vel1, vel81)
-                yield from prepare(after + turns, rolled1, table1)
-
-        run(merge(0, 0), look_ahead(1, 0))
-
-        @pl.loop(0, turns)
-        def _(turn):
-            before = jnp.maximum(turn - 1, 0)
-            one = jnp.minimum(turn + 1, turns - 1)
-            two = jnp.minimum(turn + 2, turns - 1)
-            run(fold(before, parts0))
             weave(
-                both(merge(turn, 1), look_ahead(one, 1)),
-                both(
-                    algebra(turn, merged0, mvel0, mvel80, terms0),
-                    scatter(before + turns, terms1, parts1),
-                ),
+                gather_ghosts(after, gtable0, merged0),
+                both(algebra(turn + turns, merged1, terms1), scatter(turn, terms0)),
             )
-            run(fold(before + turns, parts1))
-            weave(
-                both(merge(one, 0), look_ahead(two, 0)),
-                both(
-                    algebra(turn + turns, merged1, mvel1, mvel81, terms1),
-                    scatter(turn, terms0, parts0),
-                ),
-            )
-            give_back(turn - 1)
-
-        run(
-            scatter(2 * turns - 1, terms1, parts1),
-            fold(turns - 1, parts0),
-            fold(2 * turns - 1, parts1),
-        )
-        give_back(turns - 1)
-
-        @pl.loop(0, LISTS)
-        def _(k):
-            @pl.when(inside(me + list_offset(k)))
+
+            @pl.when(step > 0)
             def _():
-                push_back(k).wait_recv()
+                give_back(before)
+
+        last = at_turn(turns - 1)
+        run(scatter(last + turns, terms1))
+        give_back(last)
 
         total = jnp.zeros((chunks * 2 * TERM, LANES), jnp.float32)
-        for pairing in range(LISTS // 2):
+        for step in range(turns):
+            turn = (step + turns // 2) % turns
+            if step % (turns // 2) == 0:
+
+                @pl.loop(0, HOPS)
+                def _(i):
+                    k = 2 * turn + i
+
+                    @pl.when(inside(me + list_offset(k)))
+                    def _():
+                        push_back(k).wait_recv()
+
             lefts, rights = [], []
-            for k in (2 * pairing, 2 * pairing + 1):
+            for k in (2 * turn, 2 * turn + 1):
                 entry = row_of(send, k)
                 part = two_parts(jnp.where(entry >= 0, returned[k], 0.0))
                 entry16 = row_of(send, k, 16)
@@ -672,16 +650,9 @@
             pltpu.VMEM((2, WIN * ROWS, LANES), f32),
             pltpu.VMEM((20 * WIN, 8, LANES), f32),
             pltpu.VMEM((20 * WIN, 8, LANES), f32),
-            pltpu.VMEM((80, 8, LANES), f32),
-            pltpu.VMEM((80, 8, LANES), f32),
-            pltpu.VMEM((64, LANES), f32),
-            pltpu.VMEM((64, LANES), f32),
-            pltpu.VMEM((8, LANES), f32),
-            pltpu.VMEM((8, LANES), f32),
-            pltpu.VMEM((64, LANES), f32),
-            pltpu.VMEM((64, LANES), f32),
-            pltpu.VMEM((8, LANES), f32),
-            pltpu.VMEM((8, LANES), f32),
+            pltpu.VMEM((LISTS, 80, 8, LANES), f32),
+            pltpu.VMEM((LISTS, 64, LANES), f32),
+            pltpu.VMEM((LISTS, 8, LANES), f32),
             pltpu.VMEM((20, 8, LANES), f32),
             pltpu.VMEM((20, 8, LANES), f32),
             pltpu.VMEM((80, 8, LANES), f32),
@@ -690,8 +661,6 @@
             pltpu.VMEM((LISTS, 4, 8, LANES), i32),
             pltpu.VMEM((4, 8 * TERM, LANES), f32),
             pltpu.VMEM((4, 8 * TERM, LANES), f32),
-            pltpu.VMEM((2 * WIN, TERM, LANES), f32),
-            pltpu.VMEM((2 * WIN, TERM, LANES), f32),
             pltpu.VMEM(((chunks + 1) * TERM, LANES), f32),
             pltpu.VMEM((LISTS, TERM, LANES), f32),
             pltpu.VMEM((LISTS, TERM, LANES), f32),

time: 36.5 us -> 32.5 us (0.89)
  the two profiles are of different devices: /device:TPU:7 before, /device:TPU:6 now
where the time goes in v4:
time: 32.5 us; the launch traced here: 32.4 us
  Pallas kernels  29 us (89%)
  local copies, waits for them, and re-layouts  2.15 us (7%)
  between operations  1.3 us (4%)
    pallas_call x1, Pallas kernels, shards(): pl.pallas_call(make_kernel(ndev, nodes, elems), out_shape=(jax.ShapeDtype...  29 us
    unnamed x4, local copies, waits for them, and re-layouts  2.15 us

profile of v4, /device:TPU:6, one launch (start us, length us, event | category | flops | bytes accessed | tf_op | source)
XLA Modules:
  0.0 32.4 jit_solution(7306217682587994460)
XLA Ops:
  1.3 29.0 %shard_map.122 = (f32[6,3072]{1,0:T(8,128)}, f32[24,128]{1,0:T(8,128)}) custom-call(f32[6,3072]{1,0:T(8,128)} %stress_hbm.1, f32[6,3072]{1,0:T(8,128)} %dir_hbm.1, f32[6,3072]{1,0:T(8,128)} %adj_hbm.1, f32[24,128]{1,0:T(8,128)} %bitcast.23, f32[24,128]{1,0:T(8,128)} %bitcast.24, s32[512,128]{1,0:T(8,128)} %bitcast.21, f32[2048,128]{1,0:T(8,128)} %bitcast.19, ...), custom_call_target="tpu_custom_call" | custom-call | tf_op jit(solution)/shard_map/pallas_call | solution.py:625
  30.2 0.0 copy-start
  30.3 1.5 %copy.17 = f32[6,3072]{1,0:T(8,128)} copy(f32[6,3072]{1,0:T(8,128)} %get-tuple-element.8) | data formatting | bytes 147456
  31.8 0.0 copy-done
  31.8 0.6 %copy.18 = f32[3072]{0:T(1024)} copy(f32[3072]{0:T(1024)S(1)} %bitcast.22) | data formatting | bytes 24576
Async XLA Ops:
  30.2 1.6 %copy-start = (f32[24,128]{1,0:T(8,128)S(1)}, f32[24,128]{1,0:T(8,128)}, u32[]{:S(2)}) copy-start(f32[24,128]{1,0:T(8,128)} %get-tuple-element.5) | copy-start | bytes 36868

commit v5 on v3

--- a/solution.py
+++ b/solution.py
@@ -14,8 +14,9 @@
 
 LANES = 128
 ROWS = 24
-TAU, LAM, DLAM, DIR, ADJ = 0, 6, 7, 8, 16
-FIELD_ROWS = tuple(range(0, 14)) + tuple(range(16, 22))
+TAU, LAM, DLAM, DIR, ADJ = 0, 6, 7, 8, 14
+FIELDS = 20
+FIELD_ROWS = tuple(range(FIELDS))
 WIN = 3
 TERM = 8
 
@@ -123,8 +124,6 @@
         rels,
         terms0,
         terms1,
-        parts0,
-        parts1,
         acc,
         gout,
         returned,
@@ -181,14 +180,13 @@
 
         for c in range(chunks):
             cut = pl.ds(c * LANES, LANES)
-            for base in (TAU, DIR, ADJ):
-                fields[pl.ds(c * ROWS + base, 8), :] = zeros
+            fields[pl.ds(c * ROWS + 16, 8), :] = zeros
             fields[pl.ds(c * ROWS + TAU, 6), :] = 0.5 * KAPPA * stress[:, cut]
             fields[pl.ds(c * ROWS + LAM, 1), :] = relax[pl.ds(c, 1), :]
             fields[pl.ds(c * ROWS + DLAM, 1), :] = rdir[pl.ds(c, 1), :]
             fields[pl.ds(c * ROWS + DIR, 6), :] = sdir[:, cut]
             fields[pl.ds(c * ROWS + ADJ, 6), :] = adjoint[:, cut]
-        for base in (TAU, DIR, ADJ):
+        for base in (0, 8, 16):
             fields[pl.ds(chunks * ROWS + base, 8), :] = zeros
 
         def starts_of(pair):
@@ -248,8 +246,8 @@
         def push(k):
             target = me + list_offset(k)
             return pltpu.make_async_remote_copy(
-                src_ref=payload.at[k],
-                dst_ref=ghosts.at[k],
+                src_ref=payload.at[k, pl.ds(0, FIELDS)],
+                dst_ref=ghosts.at[k, pl.ds(0, FIELDS)],
                 send_sem=send_sem.at[k],
                 recv_sem=recv_sem.at[k],
                 device_id=(target,),
@@ -268,7 +266,9 @@
             )
 
         @pl.loop(0, LISTS)
-        def _(k):
+        def _(i):
+            k = (i + HOPS) % LISTS
+
             @pl.when(inside(me + list_offset(k)))
             def _():
                 push(k).start()
@@ -277,8 +277,6 @@
             acc[pl.ds(i * TERM, TERM), :] = zeros
         for i in range(LISTS):
             gout[i] = zeros
-        for i in range(2 * WIN):
-            parts0[i] = zeros
         for terms in (terms0, terms1):
             for k in range(4):
                 for g in range(8):
@@ -350,9 +348,24 @@
                 vel8[pl.ds(j, 1), :] = grad[8:9, cut]
             yield 8
 
-        run(prepare(0, rolled0, table0), prepare(turns, rolled1, table1))
-        run(gather_owned(0, table0, owned0, vel0, vel80), prepare(1, rolled0, table0))
-        run(gather_owned(turns, table1, owned1, vel1, vel81), prepare(turns + 1, rolled1, table1))
+        def at_turn(step):
+            return (step + turns // 2) % turns
+
+        def await_ghosts(turn):
+            for which in range(2):
+                k = 2 * turn + which
+
+                @pl.when(inside(me - list_offset(k)))
+                def _():
+                    push(k).wait_recv()
+
+        first, second, third = at_turn(0), at_turn(1), at_turn(2)
+        run(prepare(first, rolled0, table0), prepare(first + turns, rolled1, table1))
+        run(gather_owned(first, table0, owned0, vel0, vel80), prepare(second, rolled0, table0))
+        run(
+            gather_owned(first + turns, table1, owned1, vel1, vel81),
+            prepare(second + turns, rolled1, table1),
+        )
 
         for load in loads[8:]:
             load.wait()
@@ -423,9 +436,9 @@
                 terms[a, pl.ds(6, 8, stride=TERM), :] = score
             yield 2
 
-        def scatter(pair, terms, parts):
+        def scatter(pair, terms):
             listed = (2 * pair) % LISTS
-            for which in range(2):
+            for which, start in enumerate(starts_of(pair)):
                 lefts, rights = [], []
                 for k in range(4):
                     for j in range(groups):
@@ -454,16 +467,9 @@
                     total[16 * i : 16 * i + 8] + total[16 * i + 8 : 16 * i + 16]
                     for i in range(4)
                 ]
-                for i in range(WIN):
-                    parts[which * WIN + i] = sums[i]
-                gout[listed + which] = gout[listed + which] + sums[WIN]
-                yield 4
-
-        def fold(pair, parts):
-            for which, start in enumerate(starts_of(pair)):
                 chunk0 = start // LANES
                 shift = start % LANES
-                turned = [pltpu.roll(parts[which * WIN + i], shift, 1) for i in range(WIN)]
+                turned = [pltpu.roll(sums[i], shift, 1) for i in range(WIN)]
                 later = lane >= shift
                 for i in range(WIN + 1):
                     if i == 0:
@@ -474,23 +480,18 @@
                         add = jnp.where(later, turned[i], turned[i - 1])
                     at = pl.ds(pl.multiple_of((chunk0 + i) * TERM, TERM), TERM)
                     acc[at, :] = acc[at, :] + add
-                yield 8
+                gout[listed + which] = gout[listed + which] + sums[WIN]
+                yield 10
 
         def both(one, two):
             yield from one
             yield from two
 
-        @pl.loop(0, LISTS)
-        def _(k):
-            @pl.when(inside(me - list_offset(k)))
-            def _():
-                push(k).wait_recv()
-
         def give_back(turn):
             for which in range(2):
                 k = 2 * turn + which
 
-                @pl.when(inside(me - list_offset(k)) & (k >= 0))
+                @pl.when(inside(me - list_offset(k)))
                 def _():
                     push_back(k).start()
 
@@ -503,8 +504,7 @@
                 turn + turns, gtable1, owned1, vel1, vel81, merged1, mvel1, mvel81
             )
 
-        def look_ahead(turn, half):
-            after = jnp.minimum(turn + 1, turns - 1)
+        def look_ahead(turn, after, half):
             if half == 0:
                 yield from gather_owned(turn, table0, owned0, vel0, vel80)
                 yield from prepare(after, rolled0, table0)
@@ -512,48 +512,59 @@
                 yield from gather_owned(turn + turns, table1, owned1, vel1, vel81)
                 yield from prepare(after + turns, rolled1, table1)
 
-        run(merge(0, 0), look_ahead(1, 0))
+        await_ghosts(first)
+        run(merge(first, 0), look_ahead(second, third, 0))
 
         @pl.loop(0, turns)
-        def _(turn):
-            before = jnp.maximum(turn - 1, 0)
-            one = jnp.minimum(turn + 1, turns - 1)
-            two = jnp.minimum(turn + 2, turns - 1)
-            run(fold(before, parts0))
+        def _(step):
+            before = at_turn(jnp.maximum(step - 1, 0))
+            turn = at_turn(step)
+            one, two, three = [
+                at_turn(jnp.minimum(step + ahead, turns - 1)) for ahead in (1, 2, 3)
+            ]
+
+            @pl.when(step < turns - 1)
+            def _():
+                await_ghosts(one)
+
             weave(
-                both(merge(turn, 1), look_ahead(one, 1)),
+                both(merge(turn, 1), look_ahead(one, two, 1)),
                 both(
                     algebra(turn, merged0, mvel0, mvel80, terms0),
-                    scatter(before + turns, terms1, parts1),
+                    scatter(before + turns, terms1),
                 ),
             )
-            run(fold(before + turns, parts1))
             weave(
-                both(merge(one, 0), look_ahead(two, 0)),
+                both(merge(one, 0), look_ahead(two, three, 0)),
                 both(
                     algebra(turn + turns, merged1, mvel1, mvel81, terms1),
-                    scatter(turn, terms0, parts0),
+                    scatter(turn, terms0),
                 ),
             )
-            give_back(turn - 1)
-
-        run(
-            scatter(2 * turns - 1, terms1, parts1),
-            fold(turns - 1, parts0),
-            fold(2 * turns - 1, parts1),
-        )
-        give_back(turns - 1)
-
-        @pl.loop(0, LISTS)
-        def _(k):
-            @pl.when(inside(me + list_offset(k)))
+
+            @pl.when(step > 0)
             def _():
-                push_back(k).wait_recv()
+                give_back(before)
+
+        last = at_turn(turns - 1)
+        run(scatter(last + turns, terms1))
+        give_back(last)
 
         total = jnp.zeros((chunks * 2 * TERM, LANES), jnp.float32)
-        for pairing in range(LISTS // 2):
+        for step in range(turns):
+            turn = (step + turns // 2) % turns
+            if step % (turns // 2) == 0:
+
+                @pl.loop(0, HOPS)
+                def _(i):
+                    k = 2 * turn + i
+
+                    @pl.when(inside(me + list_offset(k)))
+                    def _():
+                        push_back(k).wait_recv()
+
             lefts, rights = [], []
-            for k in (2 * pairing, 2 * pairing + 1):
+            for k in (2 * turn, 2 * turn + 1):
                 entry = row_of(send, k)
                 part = two_parts(jnp.where(entry >= 0, returned[k], 0.0))
                 entry16 = row_of(send, k, 16)
@@ -690,8 +701,6 @@
             pltpu.VMEM((LISTS, 4, 8, LANES), i32),
             pltpu.VMEM((4, 8 * TERM, LANES), f32),
             pltpu.VMEM((4, 8 * TERM, LANES), f32),
-            pltpu.VMEM((2 * WIN, TERM, LANES), f32),
-            pltpu.VMEM((2 * WIN, TERM, LANES), f32),
             pltpu.VMEM(((chunks + 1) * TERM, LANES), f32),
             pltpu.VMEM((LISTS, TERM, LANES), f32),
             pltpu.VMEM((LISTS, TERM, LANES), f32),

time: 36.5 us -> 30.7 us (0.84)
  the two profiles are of different devices: /device:TPU:7 before, /device:TPU:6 now
where the time goes in v5:
time: 30.7 us; the launch traced here: 30.1 us
  Pallas kernels  26.7 us (87%)
  local copies, waits for them, and re-layouts  2.15 us (7%)
  between operations  1.3 us (4%)
    pallas_call x1, Pallas kernels, shards(): pl.pallas_call(make_kernel(ndev, nodes, elems), out_shape=(jax.ShapeDtype...  26.7 us
    unnamed x4, local copies, waits for them, and re-layouts  2.15 us

profile of v5, /device:TPU:6, one launch (start us, length us, event | category | flops | bytes accessed | tf_op | source)
XLA Modules:
  0.0 30.1 jit_solution(4072470548246923637)
XLA Ops:
  1.3 26.7 %shard_map.122 = (f32[6,3072]{1,0:T(8,128)}, f32[24,128]{1,0:T(8,128)}) custom-call(f32[6,3072]{1,0:T(8,128)} %stress_hbm.1, f32[6,3072]{1,0:T(8,128)} %dir_hbm.1, f32[6,3072]{1,0:T(8,128)} %adj_hbm.1, f32[24,128]{1,0:T(8,128)} %bitcast.23, f32[24,128]{1,0:T(8,128)} %bitcast.24, s32[512,128]{1,0:T(8,128)} %bitcast.21, f32[2048,128]{1,0:T(8,128)} %bitcast.19, ...), custom_call_target="tpu_custom_call" | custom-call | tf_op jit(solution)/shard_map/pallas_call | solution.py:658
  28.0 0.0 copy-start
  28.0 1.5 %copy.17 = f32[6,3072]{1,0:T(8,128)} copy(f32[6,3072]{1,0:T(8,128)} %get-tuple-element.8) | data formatting | bytes 147456
  29.5 0.0 copy-done
  29.5 0.6 %copy.18 = f32[3072]{0:T(1024)} copy(f32[3072]{0:T(1024)S(1)} %bitcast.22) | data formatting | bytes 24576
Async XLA Ops:
  28.0 1.6 %copy-start = (f32[24,128]{1,0:T(8,128)S(1)}, f32[24,128]{1,0:T(8,128)}, u32[]{:S(2)}) copy-start(f32[24,128]{1,0:T(8,128)} %get-tuple-element.5) | copy-start | bytes 36868

commit v6 on v5

--- a/solution.py
+++ b/solution.py
@@ -85,8 +85,8 @@
         grad_hbm,
         send_hbm,
         count_ref,
-        res_hbm,
-        hess_hbm,
+        acc_hbm,
+        returned,
         stress,
         sdir,
         adjoint,
@@ -97,8 +97,6 @@
         adv,
         grad,
         send,
-        res,
-        hess,
         fields,
         payload,
         ghosts,
@@ -126,7 +124,6 @@
         terms1,
         acc,
         gout,
-        returned,
         in_sem,
         out_sem,
         send_sem,
@@ -550,72 +547,61 @@
         run(scatter(last + turns, terms1))
         give_back(last)
 
-        total = jnp.zeros((chunks * 2 * TERM, LANES), jnp.float32)
-        for step in range(turns):
-            turn = (step + turns // 2) % turns
-            if step % (turns // 2) == 0:
-
-                @pl.loop(0, HOPS)
-                def _(i):
-                    k = 2 * turn + i
-
-                    @pl.when(inside(me + list_offset(k)))
-                    def _():
-                        push_back(k).wait_recv()
-
-            lefts, rights = [], []
-            for k in (2 * turn, 2 * turn + 1):
-                entry = row_of(send, k)
-                part = two_parts(jnp.where(entry >= 0, returned[k], 0.0))
-                entry16 = row_of(send, k, 16)
-                chunk = (entry16 >> 7).astype(jnp.float32).astype(jnp.bfloat16)
-                place = (entry16 & (LANES - 1)).astype(jnp.float32).astype(jnp.bfloat16)
-                lefts.append(
-                    jnp.concatenate(
-                        [
-                            jnp.where(chunk == float(i), part, zero16[:16])
-                            for i in range(chunks)
-                        ],
-                        axis=0,
-                    )
-                )
-                rights.append(factor(jnp.concatenate([place] * 8, axis=0)))
-            total = total + lax.dot_general(
-                jnp.concatenate(lefts, axis=1),
-                jnp.concatenate(rights, axis=1),
-                contract,
-                preferred_element_type=jnp.float32,
-            )
-        for c in range(chunks):
-            out = (
-                acc[pl.ds(c * TERM, TERM), :]
-                + total[16 * c : 16 * c + 8]
-                + total[16 * c + 8 : 16 * c + 16]
-            )
-            res[:, pl.ds(c * LANES, LANES)] = out[0:6]
-            hess[pl.ds(c, 1), :] = out[6:7]
-
-        stores = [
-            pltpu.make_async_copy(res, res_hbm, out_sem.at[0]),
-            pltpu.make_async_copy(hess, hess_hbm, out_sem.at[1]),
-        ]
-        for store in stores:
-            store.start()
+        store = pltpu.make_async_copy(acc.at[pl.ds(0, chunks * TERM)], acc_hbm, out_sem.at[0])
+        store.start()
 
         @pl.loop(0, LISTS)
         def _(k):
             @pl.when(inside(me + list_offset(k)))
             def _():
                 push(k).wait_send()
+                push_back(k).wait_recv()
 
             @pl.when(inside(me - list_offset(k)))
             def _():
                 push_back(k).wait_send()
 
-        for store in stores:
-            store.wait()
+        store.wait()
 
     return kernel
+
+
+def finish(acc, returned, send, res, hess):
+    chunks = hess.shape[0]
+    columns = lax.broadcasted_iota(jnp.int32, (LANES, LANES), 0).astype(jnp.bfloat16)
+    one16 = jnp.ones((LANES, LANES), jnp.bfloat16)
+    zero16 = jnp.zeros((LANES, LANES), jnp.bfloat16)
+    total = jnp.zeros((chunks * 2 * TERM, LANES), jnp.float32)
+    for pairing in range(LISTS // 2):
+        lefts, rights = [], []
+        for k in (2 * pairing, 2 * pairing + 1):
+            entry = row_of(send, k)
+            part = two_parts(jnp.where(entry >= 0, returned[k], 0.0))
+            entry16 = row_of(send, k, 16)
+            chunk = (entry16 >> 7).astype(jnp.float32).astype(jnp.bfloat16)
+            place = (entry16 & (LANES - 1)).astype(jnp.float32).astype(jnp.bfloat16)
+            lefts.append(
+                jnp.concatenate(
+                    [jnp.where(chunk == float(i), part, zero16[:16]) for i in range(chunks)],
+                    axis=0,
+                )
+            )
+            place = jnp.concatenate([place] * 8, axis=0)
+            rights.append(jnp.where(columns == place, one16, zero16))
+        total = total + lax.dot_general(
+            jnp.concatenate(lefts, axis=1),
+            jnp.concatenate(rights, axis=1),
+            (((1,), (1,)), ((), ())),
+            preferred_element_type=jnp.float32,
+        )
+    for c in range(chunks):
+        out = (
+            acc[pl.ds(c * TERM, TERM), :]
+            + total[16 * c : 16 * c + 8]
+            + total[16 * c + 8 : 16 * c + 16]
+        )
+        res[:, pl.ds(c * LANES, LANES)] = out[0:6]
+        hess[pl.ds(c, 1), :] = out[6:7]
 
 
 def shards(
@@ -655,11 +641,11 @@
         elem_count,
     )
     hbm = pl.BlockSpec(memory_space=pl.ANY)
-    res, hess = pl.pallas_call(
+    acc, returned = pl.pallas_call(
         make_kernel(ndev, nodes, elems),
         out_shape=(
-            jax.ShapeDtypeStruct((6, nodes), f32),
-            jax.ShapeDtypeStruct((chunks, LANES), f32),
+            jax.ShapeDtypeStruct((chunks * TERM, LANES), f32),
+            jax.ShapeDtypeStruct((LISTS, TERM, LANES), f32),
         ),
         in_specs=[hbm] * 10 + [pl.BlockSpec(memory_space=pltpu.SMEM)],
         out_specs=(hbm, hbm),
@@ -674,8 +660,6 @@
             pltpu.VMEM((elems // 8, LANES), f32),
             pltpu.VMEM((9, elems), f32),
             pltpu.VMEM((LISTS, LANES), i32),
-            pltpu.VMEM((6, nodes), f32),
-            pltpu.VMEM((chunks, LANES), f32),
             pltpu.VMEM(((chunks + 1) * ROWS, LANES), f32),
             pltpu.VMEM((LISTS, ROWS, LANES), f32),
             pltpu.VMEM((LISTS, ROWS, LANES), f32),
@@ -703,9 +687,8 @@
             pltpu.VMEM((4, 8 * TERM, LANES), f32),
             pltpu.VMEM(((chunks + 1) * TERM, LANES), f32),
             pltpu.VMEM((LISTS, TERM, LANES), f32),
-            pltpu.VMEM((LISTS, TERM, LANES), f32),
             pltpu.SemaphoreType.DMA((10,)),
-            pltpu.SemaphoreType.DMA((2,)),
+            pltpu.SemaphoreType.DMA((1,)),
             pltpu.SemaphoreType.DMA((LISTS,)),
             pltpu.SemaphoreType.DMA((LISTS,)),
             pltpu.SemaphoreType.DMA((LISTS,)),
@@ -717,6 +700,14 @@
             vmem_limit_bytes=62 * 1024 * 1024,
         ),
     )(*args)
+    res, hess = pl.pallas_call(
+        finish,
+        out_shape=(
+            jax.ShapeDtypeStruct((6, nodes), f32),
+            jax.ShapeDtypeStruct((chunks, LANES), f32),
+        ),
+        compiler_params=pltpu.CompilerParams(vmem_limit_bytes=62 * 1024 * 1024),
+    )(acc, returned, args[9])
     return res, hess.reshape(nodes)
 
 

time: 30.7 us -> 29.8 us (0.971)
  local copies, waits for them, and re-layouts: 2.15 us -> 0 us
  Pallas kernels: 26.7 us -> 28 us
    pallas_call x0 -> x1, Pallas kernels: none -> 2.16 us  [shards(): pl.pallas_call(finish, out_shape=(jax.ShapeDtypeStruct((6, nodes), f32),...]
    unnamed x4 -> x0, local copies, waits for them, and re-layouts: 2.15 us -> none
    pallas_call x1, Pallas kernels: 26.7 us -> 25.9 us  [shards(): pl.pallas_call(make_kernel(ndev, nodes, elems), out_shape=(jax.ShapeDtype...]
where the time goes in v6:
time: 29.8 us; the launch traced here: 29.3 us
  Pallas kernels  28 us (94%)
  between operations  1.29 us (4%)
    pallas_call x1, Pallas kernels, shards(): pl.pallas_call(make_kernel(ndev, nodes, elems), out_shape=(jax.ShapeDtype...  25.9 us
    pallas_call x1, Pallas kernels, shards(): pl.pallas_call(finish, out_shape=(jax.ShapeDtypeStruct((6, nodes), f32),...  2.16 us

profile of v6, /device:TPU:6, one launch (start us, length us, event | category | flops | bytes accessed | tf_op | source)
XLA Modules:
  0.0 29.3 jit_solution(8418719557722459881)
XLA Ops:
  1.3 25.9 %shard_map.122 = (f32[192,128]{1,0:T(8,128)}, f32[16,8,128]{2,1,0:T(8,128)}) custom-call(f32[6,3072]{1,0:T(8,128)} %stress_hbm.1, f32[6,3072]{1,0:T(8,128)} %dir_hbm.1, f32[6,3072]{1,0:T(8,128)} %adj_hbm.1, f32[24,128]{1,0:T(8,128)} %bitcast.24, f32[24,128]{1,0:T(8,128)} %bitcast.25, s32[512,128]{1,0:T(8,128)} %bitcast.21, f32[2048,128]{1,0:T(8,128)} %bitcast.19, ...), custom_call_target="tpu_custom_call" | custom-call | tf_op jit(solution)/shard_map/pallas_call | solution.py:644
  27.2 2.2 %shard_map.123 = (f32[6,3072]{1,0:T(8,128)}, f32[24,128]{1,0:T(8,128)}) custom-call(f32[192,128]{1,0:T(8,128)} %get-tuple-element.6.acc, f32[16,8,128]{2,1,0:T(8,128)} %get-tuple-element.7.returned, s32[16,128]{1,0:T(8,128)} %bitcast.23), custom_call_target="tpu_custom_call" | custom-call | tf_op jit(solution)/shard_map/pallas_call | solution.py:703

commit v7 on v6

--- a/solution.py
+++ b/solution.py
@@ -106,10 +106,13 @@
         table1,
         owned0,
         owned1,
+        owned2,
         vel0,
         vel1,
+        vel2,
         vel80,
         vel81,
+        vel82,
         mvel0,
         mvel1,
         mvel80,
@@ -221,8 +224,7 @@
         for load in loads[6:7]:
             load.wait()
 
-        @pl.loop(0, LISTS)
-        def _(k):
+        def pick(k):
             entry = row_of(send, k)
             place = entry & (LANES - 1)
             chunk = entry >> 7
@@ -236,10 +238,6 @@
                 payload[k, pl.ds(8 * t, 8), :] = picked[t]
             mark(k)
 
-        first_up = jnp.minimum(HOPS, ndev - 1 - me)
-        first_down = jnp.minimum(HOPS, me)
-        pl.semaphore_wait(barrier, first_up + first_down)
-
         def push(k):
             target = me + list_offset(k)
             return pltpu.make_async_remote_copy(
@@ -262,13 +260,27 @@
                 device_id_type=pl.DeviceIdType.MESH,
             )
 
-        @pl.loop(0, LISTS)
-        def _(i):
-            k = (i + HOPS) % LISTS
-
+        def send_off(k):
             @pl.when(inside(me + list_offset(k)))
             def _():
                 push(k).start()
+
+        early = LISTS // 4
+
+        @pl.loop(0, early)
+        def _(i):
+            pick((i + HOPS) % LISTS)
+
+        pl.semaphore_wait(barrier, jnp.minimum(HOPS, ndev - 1 - me) + jnp.minimum(HOPS, me))
+
+        @pl.loop(0, early)
+        def _(i):
+            send_off((i + HOPS) % LISTS)
+
+        @pl.loop(early, LISTS)
+        def _(i):
+            pick((i + HOPS) % LISTS)
+            send_off((i + HOPS) % LISTS)
 
         for i in range(chunks + 1):
             acc[pl.ds(i * TERM, TERM), :] = zeros
@@ -358,11 +370,12 @@
 
         first, second, third = at_turn(0), at_turn(1), at_turn(2)
         run(prepare(first, rolled0, table0), prepare(first + turns, rolled1, table1))
-        run(gather_owned(first, table0, owned0, vel0, vel80), prepare(second, rolled0, table0))
+        run(gather_owned(first, table0, owned2, vel2, vel82), prepare(second, rolled0, table0))
         run(
             gather_owned(first + turns, table1, owned1, vel1, vel81),
             prepare(second + turns, rolled1, table1),
         )
+        run(gather_owned(second, table0, owned0, vel0, vel80), prepare(third, rolled0, table0))
 
         for load in loads[8:]:
             load.wait()
@@ -510,7 +523,7 @@
                 yield from prepare(after + turns, rolled1, table1)
 
         await_ghosts(first)
-        run(merge(first, 0), look_ahead(second, third, 0))
+        run(gather_ghosts(first, gtable0, owned2, vel2, vel82, merged0, mvel0, mvel80))
 
         @pl.loop(0, turns)
         def _(step):
@@ -669,8 +682,11 @@
             pltpu.VMEM((20 * WIN, 8, LANES), f32),
             pltpu.VMEM((80, 8, LANES), f32),
             pltpu.VMEM((80, 8, LANES), f32),
+            pltpu.VMEM((80, 8, LANES), f32),
             pltpu.VMEM((64, LANES), f32),
             pltpu.VMEM((64, LANES), f32),
+            pltpu.VMEM((64, LANES), f32),
+            pltpu.VMEM((8, LANES), f32),
             pltpu.VMEM((8, LANES), f32),
             pltpu.VMEM((8, LANES), f32),
             pltpu.VMEM((64, LANES), f32),

time: 29.8 us -> 30.1 us (1.010); the launches traced: 29.3 us -> 30 us
  Pallas kernels: 28 us -> 28.7 us
    pallas_call x1, Pallas kernels: 25.9 us -> 26.6 us  [shards(): pl.pallas_call(make_kernel(ndev, nodes, elems), out_shape=(jax.ShapeDtype...]
where the time goes in v7:
time: 30.1 us; the launch traced here: 30 us
  Pallas kernels  28.7 us (95%)
  between operations  1.29 us (4%)
    pallas_call x1, Pallas kernels, shards(): pl.pallas_call(make_kernel(ndev, nodes, elems), out_shape=(jax.ShapeDtype...  26.6 us
    pallas_call x1, Pallas kernels, shards(): pl.pallas_call(finish, out_shape=(jax.ShapeDtypeStruct((6, nodes), f32),...  2.16 us

profile of v7, /device:TPU:6, one launch (start us, length us, event | category | flops | bytes accessed | tf_op | source)
XLA Modules:
  0.0 30.0 jit_solution(16539658044529455151)
XLA Ops:
  1.3 26.6 %shard_map.122 = (f32[192,128]{1,0:T(8,128)}, f32[16,8,128]{2,1,0:T(8,128)}) custom-call(f32[6,3072]{1,0:T(8,128)} %stress_hbm.1, f32[6,3072]{1,0:T(8,128)} %dir_hbm.1, f32[6,3072]{1,0:T(8,128)} %adj_hbm.1, f32[24,128]{1,0:T(8,128)} %bitcast.24, f32[24,128]{1,0:T(8,128)} %bitcast.25, s32[512,128]{1,0:T(8,128)} %bitcast.21, f32[2048,128]{1,0:T(8,128)} %bitcast.19, ...), custom_call_target="tpu_custom_call" | custom-call | tf_op jit(solution)/shard_map/pallas_call | solution.py:657
  27.8 2.2 %shard_map.123 = (f32[6,3072]{1,0:T(8,128)}, f32[24,128]{1,0:T(8,128)}) custom-call(f32[192,128]{1,0:T(8,128)} %get-tuple-element.6.acc, f32[16,8,128]{2,1,0:T(8,128)} %get-tuple-element.7.returned, s32[16,128]{1,0:T(8,128)} %bitcast.23), custom_call_target="tpu_custom_call" | custom-call | tf_op jit(solution)/shard_map/pallas_call | solution.py:719
